TPU v7x, 512 devices: a whole 4x8x8 slice. The times are simulated.
512 devices in a mesh: shard: 32 (over y, x), expert: 8 (over z), replica: 2 (over core).
Axes of the slice: x: 4, y: 8, z: 8, core: 2. Of those that a mesh axis runs over, the one named last changes fastest.
Arguments:
- momentum: float32 [32, 3584, 384], P('expert', 'shard'), may hold values from -120 to 120
- gradient: bfloat16 [32, 3584, 384], P('expert', 'shard'), may hold values from -6 to 6
- weight: bfloat16 [32, 3584, 384], P('expert', 'shard'), may hold values from -6 to 6
Outputs:
- new_momentum: float32 [32, 3584, 384], P('expert', 'shard')
- update: bfloat16 [32, 3584, 384], P('expert', 'shard')
All inputs are finite; a program needn't handle non-finite values.
Results may differ from a plain program's by a relative error of at most 0.015.
The roundings to bfloat16 on the way count: a program that leaves them out, or rounds other values in their place, can miss the bound.
Values may be sent and summed in bfloat16 or wider, within the bound.
No kernel may reach another device: no remote copies, remote signals or barrier semaphores. Data moves between devices by JAX's collectives and lax.ppermute only.
A program may use at most 64 MiB of HBM per device.

v0:
```python
import math

import jax
import jax.numpy as jnp
from jax import lax
from jax.experimental import pallas as pl
from jax.experimental.pallas import tpu as pltpu
from jax.sharding import Mesh
from jax.sharding import PartitionSpec as P

D = 3584
C = 384
ITERS = 5
BLK = 128

MOMENTUM_COEF = 0.95
NORM_EPS = 1e-07
A_COEF = 3.4445
B_COEF = -4.775
C_COEF = 2.0315
WEIGHT_DECAY = 0.1

f32 = jnp.float32
bf16 = jnp.bfloat16


def dot(a, b):
    return jnp.dot(a, b, preferred_element_type=f32)


def split(value):
    high = value.astype(bf16)
    low = (value - high.astype(f32)).astype(bf16)
    return high, low


def indices():
    row = lax.broadcasted_iota(jnp.int32, (BLK, BLK), 0)
    col = lax.broadcasted_iota(jnp.int32, (BLK, BLK), 1)
    return row, col


def packed_half(rows, half):
    gram = lax.dot_general(rows, rows, (((0,), (0,)), ((), ())), preferred_element_type=f32)
    row, col = indices()

    def block(i, j):
        return lax.slice(gram, (i, j), (i + BLK, j + BLK))

    first = jnp.where(row <= col, block(0, 0), block(BLK, BLK))
    corner = (row == BLK - 1) & (col == 0)
    spare = jnp.where(corner, block(1, BLK), block(BLK, BLK + 1))
    last = jnp.where(row <= col, block(2 * BLK, 2 * BLK), spare)
    split_block = block(0, 2 * BLK)
    return jnp.where(
        half == 0,
        jnp.concatenate([first, block(0, BLK), split_block[: BLK // 2]], axis=0),
        jnp.concatenate([split_block[BLK // 2 :], block(BLK, 2 * BLK), last], axis=0),
    )


def unpack(ref):
    row, col = indices()
    first, b01, b02, b12, last = [ref[i * BLK : (i + 1) * BLK] for i in range(5)]
    first_t, last_t = first.T, last.T
    b00 = jnp.where(row <= col, first, first_t)
    b22 = jnp.where(row <= col, last, last_t)
    corner = jnp.broadcast_to(last[BLK - 1 :, :1], (BLK, BLK))
    diagonal = jnp.where(row == 0, corner, pltpu.roll(last, 1, 1))
    b11 = jnp.where(row == col, diagonal, jnp.where(row > col, first, first_t))
    trace = jnp.where(row == col, b00 + b11 + b22, 0.0)
    gram = jnp.concatenate(
        [
            jnp.concatenate([b00, b01, b02], axis=1),
            jnp.concatenate([b01.T, b11, b12], axis=1),
            jnp.concatenate([b02.T, b12.T, b22], axis=1),
        ],
        axis=0,
    )
    return gram, jnp.sum(jnp.sum(trace, axis=1, keepdims=True), axis=0, keepdims=True)


def chain_kernel(packed_ref, own_ref, got_ref, own_out_ref, got_out_ref):
    gram, total = unpack(packed_ref)
    norm = jnp.sqrt(total) + NORM_EPS
    gram = gram / (norm * norm)
    rows = jnp.concatenate([own_ref[...], got_ref[...]], axis=0)
    iterate = (rows.astype(f32) / norm).astype(bf16)
    for iteration in range(ITERS):
        g = gram.astype(bf16)
        poly = (B_COEF * g.astype(f32) + C_COEF * dot(g, g)).astype(bf16)
        iterate = (A_COEF * iterate.astype(f32) + dot(iterate, poly)).astype(bf16)
        if iteration < ITERS - 1:
            high, low = split(gram)
            wide = jnp.concatenate([poly, poly], axis=1)
            half = A_COEF * gram + dot(wide, jnp.concatenate([high, low], axis=0))
            high, low = split(half)
            tall = jnp.concatenate([poly, poly], axis=0)
            gram = A_COEF * half + dot(jnp.concatenate([high, low], axis=1), tall)
    count = own_ref.shape[0]
    own_out_ref[...] = iterate[:count]
    got_out_ref[...] = iterate[count:]


def body(momentum, gradient, weight):
    rows = momentum.shape[1]
    members = 8
    pair = lax.axis_index("pair")
    side = lax.axis_index("side")
    first = 2 * lax.axis_index("replica")

    m = lax.dynamic_slice_in_dim(momentum, first, 2, 0)
    g = lax.dynamic_slice_in_dim(gradient, first, 2, 0)
    rounded = (MOMENTUM_COEF * m + g.astype(f32)).astype(bf16)
    new_momentum = MOMENTUM_COEF * momentum + gradient.astype(f32)
    sent = jnp.broadcast_to(rounded[None], (2, 2, rows, C)).reshape(4, rows, C)
    owned = lax.all_to_all(sent, ("pair", "side"), split_axis=0, concat_axis=0, tiled=True)
    partial = packed_half(owned.reshape(4 * rows, C), pair)
    own = lax.dynamic_index_in_dim(owned, 2 * pair + side, 0, keepdims=False)
    got = lax.dynamic_index_in_dim(owned, 2 * pair + 1 - side, 0, keepdims=False)
    pieces = partial.reshape(members, partial.shape[0] // members, BLK)
    pieces = lax.all_to_all(pieces, "y", split_axis=0, concat_axis=0, tiled=True)
    total = jnp.broadcast_to(jnp.sum(pieces, axis=0)[None], (2 * members,) + pieces.shape[1:])
    packed = lax.all_to_all(total, ("pair", "y"), split_axis=0, concat_axis=0, tiled=True)
    piece = jax.ShapeDtypeStruct((rows, C), bf16)
    own, got = pl.pallas_call(chain_kernel, out_shape=(piece, piece))(
        packed.reshape(2 * partial.shape[0], BLK), own, got
    )
    got = lax.ppermute(got, "side", [(0, 1), (1, 0)])
    both = jnp.where(side == 0, jnp.stack([own, got]), jnp.stack([got, own]))
    finished = lax.all_gather(both, "replica", axis=0, tiled=True)
    scale = 0.2 * math.sqrt(max(D, C))
    update = (scale * finished.astype(f32) + WEIGHT_DECAY * weight.astype(f32)).astype(bf16)
    return (new_momentum, update)


def solution(mesh):
    devices = mesh.devices.reshape(8, 2, 2, 8, 2)
    grid = Mesh(devices, ("y", "pair", "side", "expert", "replica"))
    placed = P("expert", ("y", "pair", "side"), None)
    return jax.shard_map(
        body,
        mesh=grid,
        in_specs=(placed, placed, placed),
        out_specs=(placed, placed),
        check_vma=False,
    )
```

profile of v0, /device:TPU:1, one launch (start us, length us, event | category | flops | bytes accessed | tf_op | source)
XLA Modules:
  0.0 66.1 jit_solution(3358178611028943277)
XLA Ops:
  0.6 1.1 %add_convert_fusion.1 = bf16[2,112,384]{2,1,0:T(8,128)(2,1)S(1)} fusion(f32[4,112,384]{2,1,0:T(8,128)} %param.3, s32[]{:T(128)S(6)} %select_n.43, bf16[4,112,384]{2,1,0:T(8,128)(2,1)} %param.4), kind=kLoop, calls=%fused_computation.3 | loop fusion | flops 344064 | bytes 688132 | tf_op jit(solution)/shard_map/convert_element_type | solution.py:114
  1.7 0.8 %broadcast_in_dim.4 = bf16[2,2,112,384]{3,2,1,0:T(8,128)(2,1)} broadcast(bf16[2,112,384]{2,1,0:T(8,128)(2,1)S(1)} %add_convert_fusion.1), dimensions={1,2,3} | broadcast | bytes 516096 | tf_op jit(solution)/shard_map/broadcast_in_dim | solution.py:116
  2.5 4.8 %all-to-all-start = ((bf16[4,112,384]{2,1,0:T(8,128)(2,1)}), bf16[4,112,384]{2,1,0:T(8,128)(2,1)S(1)}, u32[]{:S(2)}, u32[]{:S(2)}) async-start(bf16[4,112,384]{2,1,0:T(8,128)(2,1)} %bitcast), calls=%async_computation | async-start | bytes 688128 | tf_op jit(solution)/shard_map/all_to_all | solution.py:117
  7.3 6.0 %all-to-all-done = bf16[4,112,384]{2,1,0:T(8,128)(2,1)S(1)} async-done(((bf16[4,112,384]{2,1,0:T(8,128)(2,1)}), bf16[4,112,384]{2,1,0:T(8,128)(2,1)S(1)}, u32[]{:S(2)}, u32[]{:S(2)}) %all-to-all-start) | async-done | bytes 344096 | tf_op jit(solution)/shard_map/all_to_all | solution.py:117
  13.3 0.4 convolution_bitcast_fusion
  13.7 0.1 fusion
  13.8 15.4 %all_to_all.15 = f32[8,40,128]{2,1,0:T(8,128)S(1)} all-to-all(f32[8,40,128]{2,1,0:T(8,128)S(1)} %bitcast.14), channel_id=1, replica_groups=mesh['y'=8,'pair'=2,'side'=2,'expert'=8,'replica'=2] {'y'}, dimensions={0} | all-to-all | bytes 327680 | tf_op jit(solution)/shard_map/all_to_all | solution.py:122
  29.2 0.7 %broadcast_in_dim.5 = f32[16,40,128]{2,1,0:T(8,128)} broadcast(f32[40,128]{1,0:T(8,128)S(1)} %reduce_sum.9), dimensions={1,2} | broadcast | bytes 348160 | tf_op jit(solution)/shard_map/broadcast_in_dim | solution.py:123
  30.0 0.0 copy-start
  30.0 3.7 %all-to-all-start.2 = ((f32[16,40,128]{2,1,0:T(8,128)}), f32[16,40,128]{2,1,0:T(8,128)S(1)}, u32[]{:S(2)}, u32[]{:S(2)}) async-start(f32[16,40,128]{2,1,0:T(8,128)} %broadcast_in_dim.5), calls=%async_computation.2 | async-start | bytes 655360 | tf_op jit(solution)/shard_map/all_to_all | solution.py:124
  33.7 0.0 copy-start.2
  33.7 0.7 %dynamic-slice_bitcast_fusion = (bf16[112,384]{1,0:T(8,128)(2,1)}, bf16[112,384]{1,0:T(8,128)(2,1)}) fusion(bf16[4,112,384]{2,1,0:T(8,128)(2,1)S(1)} %all-to-all-done, s32[]{:T(128)S(6)} %select_n.50, s32[]{:T(128)S(6)} %select_n.49), kind=kLoop, calls=%fused_computation.6 | loop fusion | bytes 344072 | tf_op jit(solution)/shard_map/jit(dynamic_index_in_dim)/squeeze | solution.py:120
  34.4 8.9 %all-to-all-done.2 = f32[16,40,128]{2,1,0:T(8,128)S(1)} async-done(((f32[16,40,128]{2,1,0:T(8,128)}), f32[16,40,128]{2,1,0:T(8,128)S(1)}, u32[]{:S(2)}, u32[]{:S(2)}) %all-to-all-start.2) | async-done | bytes 327712 | tf_op jit(solution)/shard_map/all_to_all | solution.py:124
  43.3 0.0 copy-start.1
  43.3 0.7 %copy-done.1 = f32[16,40,128]{2,1,0:T(8,128)} copy-done((f32[16,40,128]{2,1,0:T(8,128)}, f32[16,40,128]{2,1,0:T(8,128)S(1)}, u32[]{:S(2)}) %copy-start.1) | copy-done | bytes 327704
  44.0 7.3 %shard_map.50 = (bf16[112,384]{1,0:T(8,128)(2,1)}, bf16[112,384]{1,0:T(8,128)(2,1)}) custom-call(f32[640,128]{1,0:T(8,128)} %bitcast.13, bf16[112,384]{1,0:T(8,128)(2,1)} %get-tuple-element.10.own_ref, bf16[112,384]{1,0:T(8,128)(2,1)} %get-tuple-element.9.got_ref), custom_call_target="tpu_custom_call" | custom-call | tf_op jit(solution)/shard_map/pallas_call | solution.py:126
  51.4 0.0 copy-start.4
  51.4 2.3 %collective-permute-start = (bf16[112,384]{1,0:T(8,128)(2,1)}, bf16[112,384]{1,0:T(8,128)(2,1)S(1)}, u32[]{:S(2)}, u32[]{:S(2)}) collective-permute-start(bf16[112,384]{1,0:T(8,128)(2,1)} %get-tuple-element.5), channel_id=1, source_target_pairs={{0,16},{16,0},{1,17},{17,1},{2,18},{18,2},{3,19},{19,3},{4,20},{20... | collective-permute-start | bytes 258056 | tf_op jit(solution)/shard_map/ppermute | solution.py:129
  53.7 0.0 copy-done
  53.7 0.0 copy-done.2
  53.7 0.9 %convert_add_fusion = f32[4,112,384]{2,1,0:T(8,128)} fusion(bf16[4,112,384]{2,1,0:T(8,128)(2,1)S(1)} %copy-done.2, f32[4,112,384]{2,1,0:T(8,128)S(1)} %copy-done), kind=kLoop, calls=%fused_computation.2 | loop fusion | flops 516096 | bytes 1720320 | tf_op jit(solution)/shard_map/add | solution.py:115
  54.6 2.3 %collective-permute-done = bf16[112,384]{1,0:T(8,128)(2,1)S(1)} collective-permute-done((bf16[112,384]{1,0:T(8,128)(2,1)}, bf16[112,384]{1,0:T(8,128)(2,1)S(1)}, u32[]{:S(2)}, u32[]{:S(2)}) %collective-permute-start) | collective-permute-done | bytes 86048 | tf_op jit(solution)/shard_map/ppermute | solution.py:129
  56.9 0.0 copy-done.4
  57.0 0.0 copy-start.3
  57.0 8.2 %all_gather.3 = bf16[4,112,384]{2,1,0:T(8,128)(2,1)S(1)} all-gather(bf16[2,112,384]{2,1,0:T(8,128)(2,1)S(1)} %maximum_select_fusion), channel_id=1, replica_groups=mesh['y'=8,'pair'=2,'side'=2,'expert'=8,'replica'=2] {'replica'}, dimensions={0}, use_global_device_ids=true | all-gather | bytes 516096 | tf_op jit(solution)/shard_map/all_gather | solution.py:131
  65.2 0.0 copy-done.3
  65.2 0.9 %add_convert_fusion = bf16[4,112,384]{2,1,0:T(8,128)(2,1)} fusion(bf16[4,112,384]{2,1,0:T(8,128)(2,1)S(1)} %copy-done.3, bf16[4,112,384]{2,1,0:T(8,128)(2,1)S(1)} %all_gather.3), kind=kLoop, calls=%fused_computation.1 | loop fusion | flops 1032192 | bytes 1032192 | tf_op jit(solution)/shard_map/convert_element_type | solution.py:133
  (6 shorter events, 0.1 us)
Async XLA Ops:
  2.5 10.8 %all-to-all-start = ((bf16[4,112,384]{2,1,0:T(8,128)(2,1)}), bf16[4,112,384]{2,1,0:T(8,128)(2,1)S(1)}, u32[]{:S(2)}, u32[]{:S(2)}) async-start(bf16[4,112,384]{2,1,0:T(8,128)(2,1)} %bitcast), calls=%async_computation | async-start | bytes 688128 | tf_op jit(solution)/shard_map/all_to_all | solution.py:117
  30.0 23.7 %copy-start = (f32[4,112,384]{2,1,0:T(8,128)S(1)}, f32[4,112,384]{2,1,0:T(8,128)}, u32[]{:S(2)}) copy-start(f32[4,112,384]{2,1,0:T(8,128)} %param.3) | copy-start | bytes 2064388
  30.0 13.3 %all-to-all-start.2 = ((f32[16,40,128]{2,1,0:T(8,128)}), f32[16,40,128]{2,1,0:T(8,128)S(1)}, u32[]{:S(2)}, u32[]{:S(2)}) async-start(f32[16,40,128]{2,1,0:T(8,128)} %broadcast_in_dim.5), calls=%async_computation.2 | async-start | bytes 655360 | tf_op jit(solution)/shard_map/all_to_all | solution.py:124
  33.7 20.0 %copy-start.2 = (bf16[4,112,384]{2,1,0:T(8,128)(2,1)S(1)}, bf16[4,112,384]{2,1,0:T(8,128)(2,1)}, u32[]{:S(2)}) copy-start(bf16[4,112,384]{2,1,0:T(8,128)(2,1)} %param.4) | copy-start | bytes 1032196
  43.3 0.7 %copy-start.1 = (f32[16,40,128]{2,1,0:T(8,128)}, f32[16,40,128]{2,1,0:T(8,128)S(1)}, u32[]{:S(2)}) copy-start(f32[16,40,128]{2,1,0:T(8,128)S(1)} %all-to-all-done.2) | copy-start | bytes 983044
  51.4 5.6 %copy-start.4 = (bf16[112,384]{1,0:T(8,128)(2,1)S(1)}, bf16[112,384]{1,0:T(8,128)(2,1)}, u32[]{:S(2)}) copy-start(bf16[112,384]{1,0:T(8,128)(2,1)} %get-tuple-element.4) | copy-start | bytes 258052
  51.4 5.6 %collective-permute-start = (bf16[112,384]{1,0:T(8,128)(2,1)}, bf16[112,384]{1,0:T(8,128)(2,1)S(1)}, u32[]{:S(2)}, u32[]{:S(2)}) collective-permute-start(bf16[112,384]{1,0:T(8,128)(2,1)} %get-tuple-element.5), channel_id=1, source_target_pairs={{0,16},{16,0},{1,17},{17,1},{2,18},{18,2},{3,19},{19,3},{4,20},{20... | collective-permute-start | bytes 258056 | tf_op jit(solution)/shard_map/ppermute | solution.py:129
  57.0 8.2 %copy-start.3 = (bf16[4,112,384]{2,1,0:T(8,128)(2,1)S(1)}, bf16[4,112,384]{2,1,0:T(8,128)(2,1)}, u32[]{:S(2)}) copy-start(bf16[4,112,384]{2,1,0:T(8,128)(2,1)} %param.5) | copy-start | bytes 1032196
where the time goes:
time: 66.5 us; the launch traced here: 66.1 us
  blocking collectives  23.6 us (35%)
  waiting for transfers between devices  17.2 us (26%)
  starting transfers between devices  10.8 us (16%)
  Pallas kernels  7.34 us (11%)
  other arithmetic  3.03 us (5%)
  local copies, waits for them, and re-layouts  2.95 us (4%)
  between operations  0.75 us (1%)
    all_to_all x1, blocking collectives, body(): lax.all_to_all(pieces, 'y', split_axis=0, concat_axis=0, tiled=True)  15.4 us
    all_to_all x1, waiting for transfers between devices, body(): lax.all_to_all(total, ('pair', 'y'), split_axis=0, concat_axis=0, tiled=T...  8.94 us
    all_gather x1, blocking collectives, body(): finished = lax.all_gather(both, 'replica', axis=0, tiled=True)  8.2 us
    pallas_call x1, Pallas kernels, body(): pl.pallas_call(chain_kernel, out_shape=(piece, piece))  7.34 us
    all_to_all x1, waiting for transfers between devices, body(): lax.all_to_all(sent, ('pair', 'side'), split_axis=0, concat_axis=0, tiled...  5.96 us
    all_to_all x1, starting transfers between devices, body(): lax.all_to_all(sent, ('pair', 'side'), split_axis=0, concat_axis=0, tiled...  4.84 us
    all_to_all x1, starting transfers between devices, body(): lax.all_to_all(total, ('pair', 'y'), split_axis=0, concat_axis=0, tiled=T...  3.67 us
    ppermute x1, waiting for transfers between devices, body(): got = lax.ppermute(got, 'side', [(0, 1), (1, 0)])  2.3 us
  transfers between devices with their start and end apart: 3, of which 3 were waited for; matrix products, arithmetic and copies ran while one was open for 2% of the time, Pallas kernels for 0%

commit v1 on v0

--- a/solution.py
+++ b/solution.py
@@ -80,24 +80,36 @@
     return gram, jnp.sum(jnp.sum(trace, axis=1, keepdims=True), axis=0, keepdims=True)
 
 
-def chain_kernel(packed_ref, own_ref, got_ref, own_out_ref, got_out_ref):
+def chain_kernel(packed_ref, own_ref, got_ref, own_out_ref, got_out_ref, gram_ref, x_ref):
+    count = own_ref.shape[0]
     gram, total = unpack(packed_ref)
     norm = jnp.sqrt(total) + NORM_EPS
-    gram = gram / (norm * norm)
-    rows = jnp.concatenate([own_ref[...], got_ref[...]], axis=0)
-    iterate = (rows.astype(f32) / norm).astype(bf16)
-    for iteration in range(ITERS):
-        g = gram.astype(bf16)
-        poly = (B_COEF * g.astype(f32) + C_COEF * dot(g, g)).astype(bf16)
-        iterate = (A_COEF * iterate.astype(f32) + dot(iterate, poly)).astype(bf16)
-        if iteration < ITERS - 1:
-            high, low = split(gram)
-            wide = jnp.concatenate([poly, poly], axis=1)
-            half = A_COEF * gram + dot(wide, jnp.concatenate([high, low], axis=0))
-            high, low = split(half)
-            tall = jnp.concatenate([poly, poly], axis=0)
-            gram = A_COEF * half + dot(jnp.concatenate([high, low], axis=1), tall)
-    count = own_ref.shape[0]
+    gram_ref[...] = gram / (norm * norm)
+    x_ref[:count] = (own_ref[...].astype(f32) / norm).astype(bf16)
+    x_ref[count:] = (got_ref[...].astype(f32) / norm).astype(bf16)
+
+    def polynomial():
+        g = gram_ref[...].astype(bf16)
+        return (B_COEF * g.astype(f32) + C_COEF * dot(g, g)).astype(bf16)
+
+    def advance(poly):
+        iterate = x_ref[...]
+        return (A_COEF * iterate.astype(f32) + dot(iterate, poly)).astype(bf16)
+
+    def step(iteration, carry):
+        poly = polynomial()
+        gram = gram_ref[...]
+        high, low = split(gram)
+        wide = jnp.concatenate([poly, poly], axis=1)
+        half = A_COEF * gram + dot(wide, jnp.concatenate([high, low], axis=0))
+        high, low = split(half)
+        tall = jnp.concatenate([poly, poly], axis=0)
+        gram_ref[...] = A_COEF * half + dot(jnp.concatenate([high, low], axis=1), tall)
+        x_ref[...] = advance(poly)
+        return carry
+
+    lax.fori_loop(0, ITERS - 1, step, 0)
+    iterate = advance(polynomial())
     own_out_ref[...] = iterate[:count]
     got_out_ref[...] = iterate[count:]
 
@@ -123,7 +135,11 @@
     total = jnp.broadcast_to(jnp.sum(pieces, axis=0)[None], (2 * members,) + pieces.shape[1:])
     packed = lax.all_to_all(total, ("pair", "y"), split_axis=0, concat_axis=0, tiled=True)
     piece = jax.ShapeDtypeStruct((rows, C), bf16)
-    own, got = pl.pallas_call(chain_kernel, out_shape=(piece, piece))(
+    own, got = pl.pallas_call(
+        chain_kernel,
+        out_shape=(piece, piece),
+        scratch_shapes=[pltpu.VMEM((C, C), f32), pltpu.VMEM((2 * rows, C), bf16)],
+    )(
         packed.reshape(2 * partial.shape[0], BLK), own, got
     )
     got = lax.ppermute(got, "side", [(0, 1), (1, 0)])

time: 66.5 us -> 66.5 us (level)
  no operation moved by 1% of the time
where the time goes in v1:
time: 66.5 us; the launch traced here: 66.1 us
  blocking collectives  23.6 us (35%)
  waiting for transfers between devices  17.2 us (26%)
  starting transfers between devices  10.8 us (16%)
  Pallas kernels  7.4 us (11%)
  other arithmetic  3.03 us (5%)
  local copies, waits for them, and re-layouts  2.95 us (4%)
  between operations  0.75 us (1%)
    all_to_all x1, blocking collectives, body(): lax.all_to_all(pieces, 'y', split_axis=0, concat_axis=0, tiled=True)  15.4 us
    all_to_all x1, waiting for transfers between devices, body(): lax.all_to_all(total, ('pair', 'y'), split_axis=0, concat_axis=0, tiled=T...  8.94 us
    all_gather x1, blocking collectives, body(): finished = lax.all_gather(both, 'replica', axis=0, tiled=True)  8.2 us
    pallas_call x1, Pallas kernels, body(): pl.pallas_call(chain_kernel, out_shape=(piece, piece), scratch_shapes=[pl...  7.4 us
    all_to_all x1, waiting for transfers between devices, body(): lax.all_to_all(sent, ('pair', 'side'), split_axis=0, concat_axis=0, tiled...  5.96 us
    all_to_all x1, starting transfers between devices, body(): lax.all_to_all(sent, ('pair', 'side'), split_axis=0, concat_axis=0, tiled...  4.84 us
    all_to_all x1, starting transfers between devices, body(): lax.all_to_all(total, ('pair', 'y'), split_axis=0, concat_axis=0, tiled=T...  3.67 us
    ppermute x1, starting transfers between devices, body(): got = lax.ppermute(got, 'side', [(0, 1), (1, 0)])  2.32 us
  transfers between devices with their start and end apart: 3, of which 3 were waited for; matrix products, arithmetic and copies ran while one was open for 2% of the time, Pallas kernels for 0%

profile of v1, /device:TPU:1, one launch (start us, length us, event | category | flops | bytes accessed | tf_op | source)
XLA Modules:
  0.0 66.1 jit_solution(13622363695535462629)
XLA Ops:
  0.6 1.1 %add_convert_fusion.1 = bf16[2,112,384]{2,1,0:T(8,128)(2,1)S(1)} fusion(f32[4,112,384]{2,1,0:T(8,128)} %param.3, s32[]{:T(128)S(6)} %select_n.43, bf16[4,112,384]{2,1,0:T(8,128)(2,1)} %param.4), kind=kLoop, calls=%fused_computation.3 | loop fusion | flops 344064 | bytes 688132 | tf_op jit(solution)/shard_map/convert_element_type | solution.py:126
  1.7 0.8 %broadcast_in_dim.4 = bf16[2,2,112,384]{3,2,1,0:T(8,128)(2,1)} broadcast(bf16[2,112,384]{2,1,0:T(8,128)(2,1)S(1)} %add_convert_fusion.1), dimensions={1,2,3} | broadcast | bytes 516096 | tf_op jit(solution)/shard_map/broadcast_in_dim | solution.py:128
  2.5 4.8 %all-to-all-start = ((bf16[4,112,384]{2,1,0:T(8,128)(2,1)}), bf16[4,112,384]{2,1,0:T(8,128)(2,1)S(1)}, u32[]{:S(2)}, u32[]{:S(2)}) async-start(bf16[4,112,384]{2,1,0:T(8,128)(2,1)} %bitcast), calls=%async_computation | async-start | bytes 688128 | tf_op jit(solution)/shard_map/all_to_all | solution.py:129
  7.3 6.0 %all-to-all-done = bf16[4,112,384]{2,1,0:T(8,128)(2,1)S(1)} async-done(((bf16[4,112,384]{2,1,0:T(8,128)(2,1)}), bf16[4,112,384]{2,1,0:T(8,128)(2,1)S(1)}, u32[]{:S(2)}, u32[]{:S(2)}) %all-to-all-start) | async-done | bytes 344096 | tf_op jit(solution)/shard_map/all_to_all | solution.py:129
  13.3 0.4 convolution_bitcast_fusion
  13.7 0.1 fusion
  13.8 15.4 %all_to_all.15 = f32[8,40,128]{2,1,0:T(8,128)S(1)} all-to-all(f32[8,40,128]{2,1,0:T(8,128)S(1)} %bitcast.14), channel_id=1, replica_groups=mesh['y'=8,'pair'=2,'side'=2,'expert'=8,'replica'=2] {'y'}, dimensions={0} | all-to-all | bytes 327680 | tf_op jit(solution)/shard_map/all_to_all | solution.py:134
  29.2 0.7 %broadcast_in_dim.5 = f32[16,40,128]{2,1,0:T(8,128)} broadcast(f32[40,128]{1,0:T(8,128)S(1)} %reduce_sum.9), dimensions={1,2} | broadcast | bytes 348160 | tf_op jit(solution)/shard_map/broadcast_in_dim | solution.py:135
  30.0 0.0 copy-start
  30.0 3.7 %all-to-all-start.2 = ((f32[16,40,128]{2,1,0:T(8,128)}), f32[16,40,128]{2,1,0:T(8,128)S(1)}, u32[]{:S(2)}, u32[]{:S(2)}) async-start(f32[16,40,128]{2,1,0:T(8,128)} %broadcast_in_dim.5), calls=%async_computation.2 | async-start | bytes 655360 | tf_op jit(solution)/shard_map/all_to_all | solution.py:136
  33.7 0.0 copy-start.2
  33.7 0.7 %dynamic-slice_bitcast_fusion = (bf16[112,384]{1,0:T(8,128)(2,1)}, bf16[112,384]{1,0:T(8,128)(2,1)}) fusion(bf16[4,112,384]{2,1,0:T(8,128)(2,1)S(1)} %all-to-all-done, s32[]{:T(128)S(6)} %select_n.50, s32[]{:T(128)S(6)} %select_n.49), kind=kLoop, calls=%fused_computation.6 | loop fusion | bytes 344072 | tf_op jit(solution)/shard_map/jit(dynamic_index_in_dim)/squeeze | solution.py:132
  34.4 8.9 %all-to-all-done.2 = f32[16,40,128]{2,1,0:T(8,128)S(1)} async-done(((f32[16,40,128]{2,1,0:T(8,128)}), f32[16,40,128]{2,1,0:T(8,128)S(1)}, u32[]{:S(2)}, u32[]{:S(2)}) %all-to-all-start.2) | async-done | bytes 327712 | tf_op jit(solution)/shard_map/all_to_all | solution.py:136
  43.3 0.0 copy-start.1
  43.3 0.7 %copy-done.1 = f32[16,40,128]{2,1,0:T(8,128)} copy-done((f32[16,40,128]{2,1,0:T(8,128)}, f32[16,40,128]{2,1,0:T(8,128)S(1)}, u32[]{:S(2)}) %copy-start.1) | copy-done | bytes 327704
  44.0 7.4 %shard_map.50 = (bf16[112,384]{1,0:T(8,128)(2,1)}, bf16[112,384]{1,0:T(8,128)(2,1)}) custom-call(f32[640,128]{1,0:T(8,128)} %bitcast.13, bf16[112,384]{1,0:T(8,128)(2,1)} %get-tuple-element.10.own_ref, bf16[112,384]{1,0:T(8,128)(2,1)} %get-tuple-element.9.got_ref), custom_call_target="tpu_custom_call" | custom-call | tf_op jit(solution)/shard_map/pallas_call | solution.py:138
  51.5 0.0 copy-start.4
  51.5 2.3 %collective-permute-start = (bf16[112,384]{1,0:T(8,128)(2,1)}, bf16[112,384]{1,0:T(8,128)(2,1)S(1)}, u32[]{:S(2)}, u32[]{:S(2)}) collective-permute-start(bf16[112,384]{1,0:T(8,128)(2,1)} %get-tuple-element.5), channel_id=1, source_target_pairs={{0,16},{16,0},{1,17},{17,1},{2,18},{18,2},{3,19},{19,3},{4,20},{20... | collective-permute-start | bytes 258056 | tf_op jit(solution)/shard_map/ppermute | solution.py:145
  53.8 0.0 copy-done
  53.8 0.0 copy-done.2
  53.8 0.9 %convert_add_fusion = f32[4,112,384]{2,1,0:T(8,128)} fusion(bf16[4,112,384]{2,1,0:T(8,128)(2,1)S(1)} %copy-done.2, f32[4,112,384]{2,1,0:T(8,128)S(1)} %copy-done), kind=kLoop, calls=%fused_computation.2 | loop fusion | flops 516096 | bytes 1720320 | tf_op jit(solution)/shard_map/add | solution.py:127
  54.7 2.3 %collective-permute-done = bf16[112,384]{1,0:T(8,128)(2,1)S(1)} collective-permute-done((bf16[112,384]{1,0:T(8,128)(2,1)}, bf16[112,384]{1,0:T(8,128)(2,1)S(1)}, u32[]{:S(2)}, u32[]{:S(2)}) %collective-permute-start) | collective-permute-done | bytes 86048 | tf_op jit(solution)/shard_map/ppermute | solution.py:145
  57.0 0.0 copy-done.4
  57.0 0.0 copy-start.3
  57.1 8.2 %all_gather.3 = bf16[4,112,384]{2,1,0:T(8,128)(2,1)S(1)} all-gather(bf16[2,112,384]{2,1,0:T(8,128)(2,1)S(1)} %maximum_select_fusion), channel_id=1, replica_groups=mesh['y'=8,'pair'=2,'side'=2,'expert'=8,'replica'=2] {'replica'}, dimensions={0}, use_global_device_ids=true | all-gather | bytes 516096 | tf_op jit(solution)/shard_map/all_gather | solution.py:147
  65.3 0.0 copy-done.3
  65.3 0.9 %add_convert_fusion = bf16[4,112,384]{2,1,0:T(8,128)(2,1)} fusion(bf16[4,112,384]{2,1,0:T(8,128)(2,1)S(1)} %copy-done.3, bf16[4,112,384]{2,1,0:T(8,128)(2,1)S(1)} %all_gather.3), kind=kLoop, calls=%fused_computation.1 | loop fusion | flops 1032192 | bytes 1032192 | tf_op jit(solution)/shard_map/convert_element_type | solution.py:149
  (6 shorter events, 0.1 us)
Async XLA Ops:
  2.5 10.8 %all-to-all-start = ((bf16[4,112,384]{2,1,0:T(8,128)(2,1)}), bf16[4,112,384]{2,1,0:T(8,128)(2,1)S(1)}, u32[]{:S(2)}, u32[]{:S(2)}) async-start(bf16[4,112,384]{2,1,0:T(8,128)(2,1)} %bitcast), calls=%async_computation | async-start | bytes 688128 | tf_op jit(solution)/shard_map/all_to_all | solution.py:129
  30.0 23.8 %copy-start = (f32[4,112,384]{2,1,0:T(8,128)S(1)}, f32[4,112,384]{2,1,0:T(8,128)}, u32[]{:S(2)}) copy-start(f32[4,112,384]{2,1,0:T(8,128)} %param.3) | copy-start | bytes 2064388
  30.0 13.3 %all-to-all-start.2 = ((f32[16,40,128]{2,1,0:T(8,128)}), f32[16,40,128]{2,1,0:T(8,128)S(1)}, u32[]{:S(2)}, u32[]{:S(2)}) async-start(f32[16,40,128]{2,1,0:T(8,128)} %broadcast_in_dim.5), calls=%async_computation.2 | async-start | bytes 655360 | tf_op jit(solution)/shard_map/all_to_all | solution.py:136
  33.7 20.1 %copy-start.2 = (bf16[4,112,384]{2,1,0:T(8,128)(2,1)S(1)}, bf16[4,112,384]{2,1,0:T(8,128)(2,1)}, u32[]{:S(2)}) copy-start(bf16[4,112,384]{2,1,0:T(8,128)(2,1)} %param.4) | copy-start | bytes 1032196
  43.3 0.7 %copy-start.1 = (f32[16,40,128]{2,1,0:T(8,128)}, f32[16,40,128]{2,1,0:T(8,128)S(1)}, u32[]{:S(2)}) copy-start(f32[16,40,128]{2,1,0:T(8,128)S(1)} %all-to-all-done.2) | copy-start | bytes 983044
  51.5 5.6 %copy-start.4 = (bf16[112,384]{1,0:T(8,128)(2,1)S(1)}, bf16[112,384]{1,0:T(8,128)(2,1)}, u32[]{:S(2)}) copy-start(bf16[112,384]{1,0:T(8,128)(2,1)} %get-tuple-element.4) | copy-start | bytes 258052
  51.5 5.6 %collective-permute-start = (bf16[112,384]{1,0:T(8,128)(2,1)}, bf16[112,384]{1,0:T(8,128)(2,1)S(1)}, u32[]{:S(2)}, u32[]{:S(2)}) collective-permute-start(bf16[112,384]{1,0:T(8,128)(2,1)} %get-tuple-element.5), channel_id=1, source_target_pairs={{0,16},{16,0},{1,17},{17,1},{2,18},{18,2},{3,19},{19,3},{4,20},{20... | collective-permute-start | bytes 258056 | tf_op jit(solution)/shard_map/ppermute | solution.py:145
  57.0 8.2 %copy-start.3 = (bf16[4,112,384]{2,1,0:T(8,128)(2,1)S(1)}, bf16[4,112,384]{2,1,0:T(8,128)(2,1)}, u32[]{:S(2)}) copy-start(bf16[4,112,384]{2,1,0:T(8,128)(2,1)} %param.5) | copy-start | bytes 1032196

commit v2 on v1

--- a/solution.py
+++ b/solution.py
@@ -80,13 +80,11 @@
     return gram, jnp.sum(jnp.sum(trace, axis=1, keepdims=True), axis=0, keepdims=True)
 
 
-def chain_kernel(packed_ref, own_ref, got_ref, own_out_ref, got_out_ref, gram_ref, x_ref):
-    count = own_ref.shape[0]
+def chain_kernel(packed_ref, rows_ref, out_ref, gram_ref, x_ref):
     gram, total = unpack(packed_ref)
     norm = jnp.sqrt(total) + NORM_EPS
     gram_ref[...] = gram / (norm * norm)
-    x_ref[:count] = (own_ref[...].astype(f32) / norm).astype(bf16)
-    x_ref[count:] = (got_ref[...].astype(f32) / norm).astype(bf16)
+    x_ref[...] = (rows_ref[...].astype(f32) / norm).astype(bf16)
 
     def polynomial():
         g = gram_ref[...].astype(bf16)
@@ -109,51 +107,40 @@
         return carry
 
     lax.fori_loop(0, ITERS - 1, step, 0)
-    iterate = advance(polynomial())
-    own_out_ref[...] = iterate[:count]
-    got_out_ref[...] = iterate[count:]
+    out_ref[...] = advance(polynomial())
 
 
 def body(momentum, gradient, weight):
-    rows = momentum.shape[1]
+    mats, rows, _ = momentum.shape
     members = 8
-    pair = lax.axis_index("pair")
-    side = lax.axis_index("side")
-    first = 2 * lax.axis_index("replica")
-
-    m = lax.dynamic_slice_in_dim(momentum, first, 2, 0)
-    g = lax.dynamic_slice_in_dim(gradient, first, 2, 0)
-    rounded = (MOMENTUM_COEF * m + g.astype(f32)).astype(bf16)
-    new_momentum = MOMENTUM_COEF * momentum + gradient.astype(f32)
-    sent = jnp.broadcast_to(rounded[None], (2, 2, rows, C)).reshape(4, rows, C)
-    owned = lax.all_to_all(sent, ("pair", "side"), split_axis=0, concat_axis=0, tiled=True)
-    partial = packed_half(owned.reshape(4 * rows, C), pair)
-    own = lax.dynamic_index_in_dim(owned, 2 * pair + side, 0, keepdims=False)
-    got = lax.dynamic_index_in_dim(owned, 2 * pair + 1 - side, 0, keepdims=False)
+    sent = (MOMENTUM_COEF * momentum + gradient.astype(f32)).astype(bf16)
+    owned = lax.all_to_all(sent, "x", split_axis=0, concat_axis=0, tiled=True)
+    late_momentum, late_gradient, _ = lax.optimization_barrier((momentum, gradient, sent))
+    new_momentum = MOMENTUM_COEF * late_momentum + late_gradient.astype(f32)
+    owned, new_momentum = lax.optimization_barrier((owned, new_momentum))
+    owned = owned.reshape(mats * rows, C)
+    partial = packed_half(owned, lax.axis_index("replica"))
     pieces = partial.reshape(members, partial.shape[0] // members, BLK)
     pieces = lax.all_to_all(pieces, "y", split_axis=0, concat_axis=0, tiled=True)
-    total = jnp.broadcast_to(jnp.sum(pieces, axis=0)[None], (2 * members,) + pieces.shape[1:])
-    packed = lax.all_to_all(total, ("pair", "y"), split_axis=0, concat_axis=0, tiled=True)
-    piece = jax.ShapeDtypeStruct((rows, C), bf16)
-    own, got = pl.pallas_call(
+    total = jnp.broadcast_to(jnp.sum(pieces, axis=0)[None], pieces.shape)
+    half = lax.all_to_all(total, "y", split_axis=0, concat_axis=0, tiled=True)
+    packed = lax.all_gather(half.reshape(partial.shape), "replica", axis=0, tiled=True)
+    final = pl.pallas_call(
         chain_kernel,
-        out_shape=(piece, piece),
-        scratch_shapes=[pltpu.VMEM((C, C), f32), pltpu.VMEM((2 * rows, C), bf16)],
-    )(
-        packed.reshape(2 * partial.shape[0], BLK), own, got
-    )
-    got = lax.ppermute(got, "side", [(0, 1), (1, 0)])
-    both = jnp.where(side == 0, jnp.stack([own, got]), jnp.stack([got, own]))
-    finished = lax.all_gather(both, "replica", axis=0, tiled=True)
+        out_shape=jax.ShapeDtypeStruct(owned.shape, bf16),
+        scratch_shapes=[pltpu.VMEM((C, C), f32), pltpu.VMEM(owned.shape, bf16)],
+    )(packed, owned)
+    final = final.reshape(mats, rows, C)
+    finished = lax.all_to_all(final, "x", split_axis=0, concat_axis=0, tiled=True)
     scale = 0.2 * math.sqrt(max(D, C))
     update = (scale * finished.astype(f32) + WEIGHT_DECAY * weight.astype(f32)).astype(bf16)
     return (new_momentum, update)
 
 
 def solution(mesh):
-    devices = mesh.devices.reshape(8, 2, 2, 8, 2)
-    grid = Mesh(devices, ("y", "pair", "side", "expert", "replica"))
-    placed = P("expert", ("y", "pair", "side"), None)
+    devices = mesh.devices.reshape(8, 4, 8, 2)
+    grid = Mesh(devices, ("y", "x", "expert", "replica"))
+    placed = P("expert", ("y", "x"), None)
     return jax.shard_map(
         body,
         mesh=grid,

time: 66.5 us -> 67 us (level)
  blocking collectives: 23.6 us -> 43 us
  waiting for transfers between devices: 17.2 us -> 5.02 us
  starting transfers between devices: 10.8 us -> 4.97 us
  local copies, waits for them, and re-layouts: 2.95 us -> 0.37 us
  other arithmetic: 3.03 us -> 3.99 us
  Pallas kernels: 7.4 us -> 8.17 us
    all_to_all x0 -> x2, blocking collectives: none -> 21.3 us  [the longest x1 10.8 us: body(): half = lax.all_to_all(total, 'y', split_axis=0, concat_axis=0, tiled=True)]
    all_to_all x2 -> x1, waiting for transfers between devices: 14.9 us -> 5.02 us  [body(): owned = lax.all_to_all(sent, 'x', split_axis=0, concat_axis=0, tiled=True)]
    all_to_all x2 -> x1, starting transfers between devices: 8.52 us -> 4.97 us  [body(): owned = lax.all_to_all(sent, 'x', split_axis=0, concat_axis=0, tiled=True)]
    ppermute x1 -> x0, starting transfers between devices: 2.32 us -> none  [body(): got = lax.ppermute(got, 'side', [(0, 1), (1, 0)])]
    ppermute x1 -> x0, waiting for transfers between devices: 2.28 us -> none  [body(): got = lax.ppermute(got, 'side', [(0, 1), (1, 0)])]
    all_gather x1, blocking collectives: 8.2 us -> 6.33 us  [body(): lax.all_gather(half.reshape(partial.shape), 'replica', axis=0, tiled=True)]
    broadcast_in_dim x2 -> x1, local copies, waits for them, and re-layouts: 1.51 us -> 0.01 us  [body(): total = jnp.broadcast_to(jnp.sum(pieces, axis=0)[None], pieces.shape)]
    convert_element_type x1, other arithmetic: 1.07 us -> 2.07 us  [body(): sent = (MOMENTUM_COEF * momentum + gradient.astype(f32)).astype(bf16)]
  transfers between devices with their start and end apart: 3 -> 1, of which waited for: 3 -> 1; matrix products, arithmetic and copies ran while one was open for 2% -> 1% of each run, Pallas kernels for 0% -> 0%
where the time goes in v2:
time: 67 us; the launch traced here: 66.6 us
  blocking collectives  43 us (64%)
  Pallas kernels  8.17 us (12%)
  waiting for transfers between devices  5.02 us (7%)
  starting transfers between devices  4.97 us (7%)
  other arithmetic  3.99 us (6%)
  between operations  0.69 us (1%)
    all_to_all x1, blocking collectives, body(): lax.all_to_all(pieces, 'y', split_axis=0, concat_axis=0, tiled=True)  15.4 us
    all_to_all x1, blocking collectives, body(): half = lax.all_to_all(total, 'y', split_axis=0, concat_axis=0, tiled=True)  10.8 us
    all_to_all x1, blocking collectives, body(): lax.all_to_all(final, 'x', split_axis=0, concat_axis=0, tiled=True)  10.6 us
    pallas_call x1, Pallas kernels, body(): pl.pallas_call(chain_kernel, out_shape=jax.ShapeDtypeStruct(owned.shape,...  8.17 us
    all_gather x1, blocking collectives, body(): lax.all_gather(half.reshape(partial.shape), 'replica', axis=0, tiled=True)  6.33 us
    all_to_all x1, waiting for transfers between devices, body(): owned = lax.all_to_all(sent, 'x', split_axis=0, concat_axis=0, tiled=True)  5.02 us
    all_to_all x1, starting transfers between devices, body(): owned = lax.all_to_all(sent, 'x', split_axis=0, concat_axis=0, tiled=True)  4.97 us
    convert_element_type x1, other arithmetic, body(): sent = (MOMENTUM_COEF * momentum + gradient.astype(f32)).astype(bf16)  2.07 us
  transfers between devices with their start and end apart: 1, of which 1 were waited for; matrix products, arithmetic and copies ran while one was open for 1% of the time, Pallas kernels for 0%

profile of v2, /device:TPU:1, one launch (start us, length us, event | category | flops | bytes accessed | tf_op | source)
XLA Modules:
  0.0 66.6 jit_solution(2013291051847398152)
XLA Ops:
  0.6 0.0 copy-start.2
  0.6 2.1 %add_convert_fusion.1 = bf16[4,112,384]{2,1,0:T(8,128)(2,1)} fusion(bf16[4,112,384]{2,1,0:T(8,128)(2,1)} %param.4, f32[4,112,384]{2,1,0:T(8,128)} %param.3), kind=kLoop, calls=%fused_computation.3 | loop fusion | flops 688128 | bytes 1376256 | tf_op jit(solution)/shard_map/convert_element_type | solution.py:116
  2.7 0.0 copy-start.1
  2.7 5.0 %all-to-all-start = ((bf16[4,112,384]{2,1,0:T(8,128)(2,1)}), bf16[4,112,384]{2,1,0:T(8,128)(2,1)S(1)}, u32[]{:S(2)}, u32[]{:S(2)}) async-start(bf16[4,112,384]{2,1,0:T(8,128)(2,1)} %add_convert_fusion.1), calls=%async_computation | async-start | bytes 688128 | tf_op jit(solution)/shard_map/all_to_all | solution.py:117
  7.7 0.0 copy-done.2
  7.7 0.0 copy-done.1
  7.7 0.9 %convert_add_fusion = f32[4,112,384]{2,1,0:T(8,128)} fusion(bf16[4,112,384]{2,1,0:T(8,128)(2,1)S(1)} %copy-done.2, f32[4,112,384]{2,1,0:T(8,128)S(1)} %copy-done.1), kind=kLoop, calls=%fused_computation.2 | loop fusion | flops 516096 | bytes 1720320 | tf_op jit(solution)/shard_map/add | solution.py:119
  8.6 5.0 %all-to-all-done = bf16[4,112,384]{2,1,0:T(8,128)(2,1)S(1)} async-done(((bf16[4,112,384]{2,1,0:T(8,128)(2,1)}), bf16[4,112,384]{2,1,0:T(8,128)(2,1)S(1)}, u32[]{:S(2)}, u32[]{:S(2)}) %all-to-all-start) | async-done | bytes 344096 | tf_op jit(solution)/shard_map/all_to_all | solution.py:117
  13.7 0.0 copy-start
  13.7 0.4 convolution_bitcast_fusion
  14.0 0.3 copy-done
  14.4 0.1 fusion
  14.5 15.4 %all_to_all.20 = f32[8,40,128]{2,1,0:T(8,128)S(1)} all-to-all(f32[8,40,128]{2,1,0:T(8,128)S(1)} %bitcast.10), channel_id=1, replica_groups=mesh['y'=8,'x'=4,'expert'=8,'replica'=2] {'y'}, dimensions={0} | all-to-all | bytes 327680 | tf_op jit(solution)/shard_map/all_to_all | solution.py:124
  29.9 10.8 %all_to_all.21 = f32[8,40,128]{2,1,0:T(8,128)S(1)} all-to-all(f32[8,40,128]{2,1,0:T(8,128)S(1)} %broadcast_in_dim.2), channel_id=1, replica_groups=mesh['y'=8,'x'=4,'expert'=8,'replica'=2] {'y'}, dimensions={0} | all-to-all | bytes 327680 | tf_op jit(solution)/shard_map/all_to_all | solution.py:126
  40.7 6.3 %all_gather.3.packed_ref = f32[640,128]{1,0:T(8,128)} all-gather(f32[320,128]{1,0:T(8,128)S(1)} %bitcast.11), channel_id=1, replica_groups=mesh['y'=8,'x'=4,'expert'=8,'replica'=2] {'replica'}, dimensions={0}, use_global_device_ids=true | all-gather | bytes 491520 | tf_op jit(solution)/shard_map/all_gather | solution.py:127
  47.0 8.2 %shard_map.50 = bf16[448,384]{1,0:T(8,128)(2,1)} custom-call(f32[640,128]{1,0:T(8,128)} %all_gather.3.packed_ref, bf16[448,384]{1,0:T(8,128)(2,1)} %bitcast.8), custom_call_target="tpu_custom_call" | custom-call | tf_op jit(solution)/shard_map/pallas_call | solution.py:128
  55.2 0.0 copy-start.3
  55.2 10.6 %all_to_all.22 = bf16[4,112,384]{2,1,0:T(8,128)(2,1)S(1)} all-to-all(bf16[4,112,384]{2,1,0:T(8,128)(2,1)} %bitcast.9), channel_id=1, replica_groups=mesh['y'=8,'x'=4,'expert'=8,'replica'=2] {'x'}, dimensions={0} | all-to-all | bytes 688128 | tf_op jit(solution)/shard_map/all_to_all | solution.py:134
  65.8 0.0 copy-done.3
  65.8 0.9 %add_convert_fusion = bf16[4,112,384]{2,1,0:T(8,128)(2,1)} fusion(bf16[4,112,384]{2,1,0:T(8,128)(2,1)S(1)} %copy-done.3, bf16[4,112,384]{2,1,0:T(8,128)(2,1)S(1)} %all_to_all.22), kind=kLoop, calls=%fused_computation.1 | loop fusion | flops 1032192 | bytes 1032192 | tf_op jit(solution)/shard_map/convert_element_type | solution.py:136
  (6 shorter events, 0.1 us)
Async XLA Ops:
  0.6 7.1 %copy-start.2 = (bf16[4,112,384]{2,1,0:T(8,128)(2,1)S(1)}, bf16[4,112,384]{2,1,0:T(8,128)(2,1)}, u32[]{:S(2)}) copy-start(bf16[4,112,384]{2,1,0:T(8,128)(2,1)} %param.4) | copy-start | bytes 1032196
  2.7 5.0 %copy-start.1 = (f32[4,112,384]{2,1,0:T(8,128)S(1)}, f32[4,112,384]{2,1,0:T(8,128)}, u32[]{:S(2)}) copy-start(f32[4,112,384]{2,1,0:T(8,128)} %param.3) | copy-start | bytes 2064388
  2.7 10.9 %all-to-all-start = ((bf16[4,112,384]{2,1,0:T(8,128)(2,1)}), bf16[4,112,384]{2,1,0:T(8,128)(2,1)S(1)}, u32[]{:S(2)}, u32[]{:S(2)}) async-start(bf16[4,112,384]{2,1,0:T(8,128)(2,1)} %add_convert_fusion.1), calls=%async_computation | async-start | bytes 688128 | tf_op jit(solution)/shard_map/all_to_all | solution.py:117
  13.7 0.7 %copy-start = (bf16[4,112,384]{2,1,0:T(8,128)(2,1)}, bf16[4,112,384]{2,1,0:T(8,128)(2,1)S(1)}, u32[]{:S(2)}) copy-start(bf16[4,112,384]{2,1,0:T(8,128)(2,1)S(1)} %all-to-all-done) | copy-start | bytes 1032196
  55.2 10.6 %copy-start.3 = (bf16[4,112,384]{2,1,0:T(8,128)(2,1)S(1)}, bf16[4,112,384]{2,1,0:T(8,128)(2,1)}, u32[]{:S(2)}) copy-start(bf16[4,112,384]{2,1,0:T(8,128)(2,1)} %param.5) | copy-start | bytes 1032196

commit v3 on v1

--- a/solution.py
+++ b/solution.py
@@ -40,7 +40,7 @@
     return row, col
 
 
-def packed_half(rows, half):
+def pack(rows):
     gram = lax.dot_general(rows, rows, (((0,), (0,)), ((), ())), preferred_element_type=f32)
     row, col = indices()
 
@@ -51,11 +51,8 @@
     corner = (row == BLK - 1) & (col == 0)
     spare = jnp.where(corner, block(1, BLK), block(BLK, BLK + 1))
     last = jnp.where(row <= col, block(2 * BLK, 2 * BLK), spare)
-    split_block = block(0, 2 * BLK)
-    return jnp.where(
-        half == 0,
-        jnp.concatenate([first, block(0, BLK), split_block[: BLK // 2]], axis=0),
-        jnp.concatenate([split_block[BLK // 2 :], block(BLK, 2 * BLK), last], axis=0),
+    return jnp.concatenate(
+        [first, block(0, BLK), block(0, 2 * BLK), block(BLK, 2 * BLK), last], axis=0
     )
 
 
@@ -116,32 +113,29 @@
 
 def body(momentum, gradient, weight):
     rows = momentum.shape[1]
-    members = 8
-    pair = lax.axis_index("pair")
+    members = 16
     side = lax.axis_index("side")
     first = 2 * lax.axis_index("replica")
 
-    m = lax.dynamic_slice_in_dim(momentum, first, 2, 0)
-    g = lax.dynamic_slice_in_dim(gradient, first, 2, 0)
-    rounded = (MOMENTUM_COEF * m + g.astype(f32)).astype(bf16)
+    def rounded(index):
+        m = lax.dynamic_index_in_dim(momentum, index, 0, keepdims=False)
+        g = lax.dynamic_index_in_dim(gradient, index, 0, keepdims=False)
+        return (MOMENTUM_COEF * m + g.astype(f32)).astype(bf16)
+
+    got = lax.ppermute(rounded(first + 1 - side), "side", [(0, 1), (1, 0)])
+    own = rounded(first + side)
     new_momentum = MOMENTUM_COEF * momentum + gradient.astype(f32)
-    sent = jnp.broadcast_to(rounded[None], (2, 2, rows, C)).reshape(4, rows, C)
-    owned = lax.all_to_all(sent, ("pair", "side"), split_axis=0, concat_axis=0, tiled=True)
-    partial = packed_half(owned.reshape(4 * rows, C), pair)
-    own = lax.dynamic_index_in_dim(owned, 2 * pair + side, 0, keepdims=False)
-    got = lax.dynamic_index_in_dim(owned, 2 * pair + 1 - side, 0, keepdims=False)
+    partial = pack(jnp.concatenate([own, got], axis=0))
     pieces = partial.reshape(members, partial.shape[0] // members, BLK)
-    pieces = lax.all_to_all(pieces, "y", split_axis=0, concat_axis=0, tiled=True)
-    total = jnp.broadcast_to(jnp.sum(pieces, axis=0)[None], (2 * members,) + pieces.shape[1:])
+    pieces = lax.all_to_all(pieces, ("pair", "y"), split_axis=0, concat_axis=0, tiled=True)
+    total = jnp.broadcast_to(jnp.sum(pieces, axis=0)[None], pieces.shape)
     packed = lax.all_to_all(total, ("pair", "y"), split_axis=0, concat_axis=0, tiled=True)
     piece = jax.ShapeDtypeStruct((rows, C), bf16)
     own, got = pl.pallas_call(
         chain_kernel,
         out_shape=(piece, piece),
         scratch_shapes=[pltpu.VMEM((C, C), f32), pltpu.VMEM((2 * rows, C), bf16)],
-    )(
-        packed.reshape(2 * partial.shape[0], BLK), own, got
-    )
+    )(packed.reshape(partial.shape), own, got)
     got = lax.ppermute(got, "side", [(0, 1), (1, 0)])
     both = jnp.where(side == 0, jnp.stack([own, got]), jnp.stack([got, own]))
     finished = lax.all_gather(both, "replica", axis=0, tiled=True)

time: 66.5 us -> 65.4 us (0.983)
  blocking collectives: 23.6 us -> 42.6 us
  waiting for transfers between devices: 17.2 us -> 3.52 us
  starting transfers between devices: 10.8 us -> 6.88 us
  local copies, waits for them, and re-layouts: 2.95 us -> 0.39 us
    all_to_all x1 -> x2, blocking collectives: 15.4 us -> 36.1 us  [the longest x1 19 us: body(): lax.all_to_all(pieces, ('pair', 'y'), split_axis=0, concat_axis=0, tiled=...]
    all_to_all x2 -> x0, waiting for transfers between devices: 14.9 us -> none  [the longest x1 8.94 us: body(): lax.all_to_all(total, ('pair', 'y'), split_axis=0, concat_axis=0, tiled=T...]
    all_to_all x2 -> x0, starting transfers between devices: 8.52 us -> none  [the longest x1 4.84 us: body(): lax.all_to_all(sent, ('pair', 'side'), split_axis=0, concat_axis=0, tiled...]
    ppermute x0 -> x1, starting transfers between devices: none -> 3.95 us  [body(): got = lax.ppermute(rounded(first + 1 - side), 'side', [(0, 1), (1, 0)])]
    ppermute x0 -> x1, waiting for transfers between devices: none -> 1.85 us  [body(): got = lax.ppermute(rounded(first + 1 - side), 'side', [(0, 1), (1, 0)])]
    all_gather x1, blocking collectives: 8.2 us -> 6.47 us  [body(): finished = lax.all_gather(both, 'replica', axis=0, tiled=True)]
    broadcast_in_dim x2 -> x1, local copies, waits for them, and re-layouts: 1.51 us -> 0.02 us  [body(): total = jnp.broadcast_to(jnp.sum(pieces, axis=0)[None], pieces.shape)]
    squeeze x1 -> x0, local copies, waits for them, and re-layouts: 0.69 us -> none  [body(): lax.dynamic_index_in_dim(owned, 2 * pair + 1 - side, 0, keepdims=False)]
  transfers between devices with their start and end apart: 3 -> 2, of which waited for: 3 -> 2; matrix products, arithmetic and copies ran while one was open for 2% -> 1% of each run, Pallas kernels for 0% -> 0%
where the time goes in v3:
time: 65.4 us; the launch traced here: 65 us
  blocking collectives  42.6 us (65%)
  Pallas kernels  7.47 us (11%)
  starting transfers between devices  6.88 us (11%)
  waiting for transfers between devices  3.52 us (5%)
  other arithmetic  3.12 us (5%)
  between operations  0.76 us (1%)
    all_to_all x1, blocking collectives, body(): lax.all_to_all(pieces, ('pair', 'y'), split_axis=0, concat_axis=0, tiled=...  19 us
    all_to_all x1, blocking collectives, body(): lax.all_to_all(total, ('pair', 'y'), split_axis=0, concat_axis=0, tiled=T...  17.1 us
    pallas_call x1, Pallas kernels, body(): pl.pallas_call(chain_kernel, out_shape=(piece, piece), scratch_shapes=[pl...  7.47 us
    all_gather x1, blocking collectives, body(): finished = lax.all_gather(both, 'replica', axis=0, tiled=True)  6.47 us
    ppermute x1, starting transfers between devices, body(): got = lax.ppermute(rounded(first + 1 - side), 'side', [(0, 1), (1, 0)])  3.95 us
    ppermute x1, starting transfers between devices, body(): got = lax.ppermute(got, 'side', [(0, 1), (1, 0)])  2.93 us
    ppermute x1, waiting for transfers between devices, body(): got = lax.ppermute(rounded(first + 1 - side), 'side', [(0, 1), (1, 0)])  1.85 us
    ppermute x1, waiting for transfers between devices, body(): got = lax.ppermute(got, 'side', [(0, 1), (1, 0)])  1.67 us
  transfers between devices with their start and end apart: 2, of which 2 were waited for; matrix products, arithmetic and copies ran while one was open for 1% of the time, Pallas kernels for 0%

profile of v3, /device:TPU:1, one launch (start us, length us, event | category | flops | bytes accessed | tf_op | source)
XLA Modules:
  0.0 65.0 jit_solution(13649126396082557624)
XLA Ops:
  0.6 1.1 %fusion.4 = (bf16[112,384]{1,0:T(8,128)(2,1)S(1)}, bf16[112,384]{1,0:T(8,128)(2,1)S(1)}) fusion(f32[4,112,384]{2,1,0:T(8,128)} %param.3, s32[]{:T(128)S(6)} %select_n.29, bf16[4,112,384]{2,1,0:T(8,128)(2,1)} %param.4, s32[]{:T(128)S(6)} %select_n.30), kind=kLoop, calls=%fused_computation.10 | loop fusion | flops 344064 | bytes 688136 | tf_op jit(solution)/shard_map/convert_element_type | solution.py:123
  1.8 0.0 copy-start.2
  1.8 3.9 %collective-permute-start = (bf16[112,384]{1,0:T(8,128)(2,1)S(1)}, bf16[112,384]{1,0:T(8,128)(2,1)S(1)}, u32[]{:S(2)}, u32[]{:S(2)}) collective-permute-start(bf16[112,384]{1,0:T(8,128)(2,1)S(1)} %get-tuple-element.7), channel_id=1, source_target_pairs={{0,16},{16,0},{1,17},{17,1},{2,18},{18,2},{3,19},{19,3},{4,20},{20... | collective-permute-start | bytes 258056 | tf_op jit(solution)/shard_map/ppermute | solution.py:125
  5.8 1.8 %collective-permute-done.got_ref = bf16[112,384]{1,0:T(8,128)(2,1)S(1)} collective-permute-done((bf16[112,384]{1,0:T(8,128)(2,1)S(1)}, bf16[112,384]{1,0:T(8,128)(2,1)S(1)}, u32[]{:S(2)}, u32[]{:S(2)}) %collective-permute-start) | collective-permute-done | bytes 86048 | tf_op jit(solution)/shard_map/ppermute | solution.py:125
  7.6 0.0 copy-start.4
  7.6 0.3 fusion
  7.9 0.0 copy-done.2
  7.9 0.3 copy-done.4
  8.3 0.1 slice_select_fusion.1
  8.4 19.0 %all_to_all.10 = f32[16,40,128]{2,1,0:T(8,128)S(1)} all-to-all(f32[16,40,128]{2,1,0:T(8,128)S(1)} %bitcast.9), channel_id=1, replica_groups=mesh['y'=8,'pair'=2,'side'=2,'expert'=8,'replica'=2] {'pair','y'}, dimensions={0} | all-to-all | bytes 655360 | tf_op jit(solution)/shard_map/all_to_all | solution.py:130
  27.4 0.0 copy-start
  27.5 17.1 %all_to_all.11 = f32[16,40,128]{2,1,0:T(8,128)} all-to-all(f32[16,40,128]{2,1,0:T(8,128)S(1)} %broadcast_in_dim.2), channel_id=1, replica_groups=mesh['y'=8,'pair'=2,'side'=2,'expert'=8,'replica'=2] {'pair','y'}, dimensions={0} | all-to-all | bytes 655360 | tf_op jit(solution)/shard_map/all_to_all | solution.py:132
  44.6 0.0 copy-start.1
  44.6 7.5 %shard_map.50 = (bf16[112,384]{1,0:T(8,128)(2,1)}, bf16[112,384]{1,0:T(8,128)(2,1)}) custom-call(f32[640,128]{1,0:T(8,128)} %bitcast.8, bf16[112,384]{1,0:T(8,128)(2,1)} %copy-done.2, bf16[112,384]{1,0:T(8,128)(2,1)} %copy-done.4), custom_call_target="tpu_custom_call" | custom-call | tf_op jit(solution)/shard_map/pallas_call | solution.py:134
  52.1 0.0 copy-start.5
  52.1 2.9 %collective-permute-start.1 = (bf16[112,384]{1,0:T(8,128)(2,1)}, bf16[112,384]{1,0:T(8,128)(2,1)S(1)}, u32[]{:S(2)}, u32[]{:S(2)}) collective-permute-start(bf16[112,384]{1,0:T(8,128)(2,1)} %get-tuple-element.5), channel_id=1, source_target_pairs={{0,16},{16,0},{1,17},{17,1},{2,18},{18,2},{3,19},{19,3},{4,20},{20... | collective-permute-start | bytes 258056 | tf_op jit(solution)/shard_map/ppermute | solution.py:139
  55.0 0.0 copy-done
  55.1 0.0 copy-done.1
  55.1 0.9 %convert_add_fusion = f32[4,112,384]{2,1,0:T(8,128)} fusion(bf16[4,112,384]{2,1,0:T(8,128)(2,1)S(1)} %copy-done.1, f32[4,112,384]{2,1,0:T(8,128)S(1)} %copy-done), kind=kLoop, calls=%fused_computation.1 | loop fusion | flops 516096 | bytes 1720320 | tf_op jit(solution)/shard_map/add | solution.py:127
  56.0 1.7 %collective-permute-done.1 = bf16[112,384]{1,0:T(8,128)(2,1)S(1)} collective-permute-done((bf16[112,384]{1,0:T(8,128)(2,1)}, bf16[112,384]{1,0:T(8,128)(2,1)S(1)}, u32[]{:S(2)}, u32[]{:S(2)}) %collective-permute-start.1) | collective-permute-done | bytes 86048 | tf_op jit(solution)/shard_map/ppermute | solution.py:139
  57.7 0.0 copy-done.5
  57.7 0.0 copy-start.3
  57.7 6.5 %all_gather.3 = bf16[4,112,384]{2,1,0:T(8,128)(2,1)S(1)} all-gather(bf16[2,112,384]{2,1,0:T(8,128)(2,1)S(1)} %maximum_select_fusion), channel_id=1, replica_groups=mesh['y'=8,'pair'=2,'side'=2,'expert'=8,'replica'=2] {'replica'}, dimensions={0}, use_global_device_ids=true | all-gather | bytes 516096 | tf_op jit(solution)/shard_map/all_gather | solution.py:141
  64.2 0.0 copy-done.3
  64.2 0.9 %add_convert_fusion = bf16[4,112,384]{2,1,0:T(8,128)(2,1)} fusion(bf16[4,112,384]{2,1,0:T(8,128)(2,1)S(1)} %copy-done.3, bf16[4,112,384]{2,1,0:T(8,128)(2,1)S(1)} %all_gather.3), kind=kLoop, calls=%fused_computation | loop fusion | flops 1032192 | bytes 1032192 | tf_op jit(solution)/shard_map/convert_element_type | solution.py:143
  (6 shorter events, 0.1 us)
Async XLA Ops:
  1.8 6.1 %copy-start.2 = (bf16[112,384]{1,0:T(8,128)(2,1)}, bf16[112,384]{1,0:T(8,128)(2,1)S(1)}, u32[]{:S(2)}) copy-start(bf16[112,384]{1,0:T(8,128)(2,1)S(1)} %get-tuple-element.6.own_ref) | copy-start | bytes 258052
  1.8 5.8 %collective-permute-start = (bf16[112,384]{1,0:T(8,128)(2,1)S(1)}, bf16[112,384]{1,0:T(8,128)(2,1)S(1)}, u32[]{:S(2)}, u32[]{:S(2)}) collective-permute-start(bf16[112,384]{1,0:T(8,128)(2,1)S(1)} %get-tuple-element.7), channel_id=1, source_target_pairs={{0,16},{16,0},{1,17},{17,1},{2,18},{18,2},{3,19},{19,3},{4,20},{20... | collective-permute-start | bytes 258056 | tf_op jit(solution)/shard_map/ppermute | solution.py:125
  7.6 0.6 copy-start.4
  27.4 27.6 %copy-start = (f32[4,112,384]{2,1,0:T(8,128)S(1)}, f32[4,112,384]{2,1,0:T(8,128)}, u32[]{:S(2)}) copy-start(f32[4,112,384]{2,1,0:T(8,128)} %param.3) | copy-start | bytes 2064388
  44.6 10.4 %copy-start.1 = (bf16[4,112,384]{2,1,0:T(8,128)(2,1)S(1)}, bf16[4,112,384]{2,1,0:T(8,128)(2,1)}, u32[]{:S(2)}) copy-start(bf16[4,112,384]{2,1,0:T(8,128)(2,1)} %param.4) | copy-start | bytes 1032196
  52.1 5.6 %copy-start.5 = (bf16[112,384]{1,0:T(8,128)(2,1)S(1)}, bf16[112,384]{1,0:T(8,128)(2,1)}, u32[]{:S(2)}) copy-start(bf16[112,384]{1,0:T(8,128)(2,1)} %get-tuple-element.4) | copy-start | bytes 258052
  52.1 5.6 %collective-permute-start.1 = (bf16[112,384]{1,0:T(8,128)(2,1)}, bf16[112,384]{1,0:T(8,128)(2,1)S(1)}, u32[]{:S(2)}, u32[]{:S(2)}) collective-permute-start(bf16[112,384]{1,0:T(8,128)(2,1)} %get-tuple-element.5), channel_id=1, source_target_pairs={{0,16},{16,0},{1,17},{17,1},{2,18},{18,2},{3,19},{19,3},{4,20},{20... | collective-permute-start | bytes 258056 | tf_op jit(solution)/shard_map/ppermute | solution.py:139
  57.7 6.5 %copy-start.3 = (bf16[4,112,384]{2,1,0:T(8,128)(2,1)S(1)}, bf16[4,112,384]{2,1,0:T(8,128)(2,1)}, u32[]{:S(2)}) copy-start(bf16[4,112,384]{2,1,0:T(8,128)(2,1)} %param.5) | copy-start | bytes 1032196

commit v4 on v3

--- a/solution.py
+++ b/solution.py
@@ -117,13 +117,15 @@
     side = lax.axis_index("side")
     first = 2 * lax.axis_index("replica")
 
-    def rounded(index):
-        m = lax.dynamic_index_in_dim(momentum, index, 0, keepdims=False)
-        g = lax.dynamic_index_in_dim(gradient, index, 0, keepdims=False)
+    def rounded(new, old, index):
+        m = lax.dynamic_index_in_dim(old, index, 0, keepdims=False)
+        g = lax.dynamic_index_in_dim(new, index, 0, keepdims=False)
         return (MOMENTUM_COEF * m + g.astype(f32)).astype(bf16)
 
-    got = lax.ppermute(rounded(first + 1 - side), "side", [(0, 1), (1, 0)])
-    own = rounded(first + side)
+    sent = rounded(gradient, momentum, first + 1 - side)
+    later = lax.optimization_barrier((gradient, momentum, sent))
+    got = lax.ppermute(sent, "side", [(0, 1), (1, 0)])
+    own = rounded(later[0], later[1], first + side)
     new_momentum = MOMENTUM_COEF * momentum + gradient.astype(f32)
     partial = pack(jnp.concatenate([own, got], axis=0))
     pieces = partial.reshape(members, partial.shape[0] // members, BLK)

time: 65.4 us -> 65.2 us (level)
  waiting for transfers between devices: 3.52 us -> 2.54 us
  other arithmetic: 3.12 us -> 3.97 us
    ppermute x1, waiting for transfers between devices: 1.85 us -> 0.87 us  [body(): got = lax.ppermute(sent, 'side', [(0, 1), (1, 0)])]
    convert_element_type x1 -> x2, other arithmetic: 1.15 us -> 1.99 us  [rounded(): return (MOMENTUM_COEF * m + g.astype(f32)).astype(bf16)]
  transfers between devices with their start and end apart: 2 -> 2, of which waited for: 2 -> 2; matrix products, arithmetic and copies ran while one was open for 1% -> 3% of each run, Pallas kernels for 0% -> 0%
where the time goes in v4:
time: 65.2 us; the launch traced here: 64.9 us
  blocking collectives  42.6 us (65%)
  Pallas kernels  7.4 us (11%)
  starting transfers between devices  6.89 us (11%)
  other arithmetic  3.97 us (6%)
  waiting for transfers between devices  2.54 us (4%)
  between operations  0.78 us (1%)
    all_to_all x1, blocking collectives, body(): lax.all_to_all(pieces, ('pair', 'y'), split_axis=0, concat_axis=0, tiled=...  19 us
    all_to_all x1, blocking collectives, body(): lax.all_to_all(total, ('pair', 'y'), split_axis=0, concat_axis=0, tiled=T...  17.1 us
    pallas_call x1, Pallas kernels, body(): pl.pallas_call(chain_kernel, out_shape=(piece, piece), scratch_shapes=[pl...  7.4 us
    all_gather x1, blocking collectives, body(): finished = lax.all_gather(both, 'replica', axis=0, tiled=True)  6.47 us
    ppermute x1, starting transfers between devices, body(): got = lax.ppermute(sent, 'side', [(0, 1), (1, 0)])  3.95 us
    ppermute x1, starting transfers between devices, body(): got = lax.ppermute(got, 'side', [(0, 1), (1, 0)])  2.94 us
    convert_element_type x2, other arithmetic, rounded(): return (MOMENTUM_COEF * m + g.astype(f32)).astype(bf16)  1.99 us
    ppermute x1, waiting for transfers between devices, body(): got = lax.ppermute(got, 'side', [(0, 1), (1, 0)])  1.67 us
  transfers between devices with their start and end apart: 2, of which 2 were waited for; matrix products, arithmetic and copies ran while one was open for 3% of the time, Pallas kernels for 0%

profile of v4, /device:TPU:1, one launch (start us, length us, event | category | flops | bytes accessed | tf_op | source)
XLA Modules:
  0.0 64.9 jit_solution(10393689370282957942)
XLA Ops:
  0.6 0.0 copy-start.1
  0.7 1.0 %fusion.4 = bf16[112,384]{1,0:T(8,128)(2,1)S(1)} fusion(f32[4,112,384]{2,1,0:T(8,128)} %param.3, s32[]{:T(128)S(6)} %select_n.29, bf16[4,112,384]{2,1,0:T(8,128)(2,1)} %param.4), kind=kLoop, calls=%fused_computation.10 | loop fusion | flops 172032 | bytes 344068 | tf_op jit(solution)/shard_map/convert_element_type | solution.py:123
  1.7 3.9 %collective-permute-start = (bf16[112,384]{1,0:T(8,128)(2,1)S(1)}, bf16[112,384]{1,0:T(8,128)(2,1)S(1)}, u32[]{:S(2)}, u32[]{:S(2)}) collective-permute-start(bf16[112,384]{1,0:T(8,128)(2,1)S(1)} %fusion.4), channel_id=1, source_target_pairs={{0,16},{16,0},{1,17},{17,1},{2,18},{18,2},{3,19},{19,3},{4,20},{20... | collective-permute-start | bytes 258056 | tf_op jit(solution)/shard_map/ppermute | solution.py:127
  5.7 0.0 copy-done.1
  5.7 1.0 %fusion.5.own_ref = bf16[112,384]{1,0:T(8,128)(2,1)S(1)} fusion(f32[4,112,384]{2,1,0:T(8,128)} %param.3, s32[]{:T(128)S(6)} %select_n.30, bf16[4,112,384]{2,1,0:T(8,128)(2,1)S(1)} %copy-done.1), kind=kLoop, calls=%fused_computation.11 | loop fusion | flops 172032 | bytes 344068 | tf_op jit(solution)/shard_map/convert_element_type | solution.py:123
  6.6 0.0 copy-start.2
  6.6 0.9 %collective-permute-done.got_ref = bf16[112,384]{1,0:T(8,128)(2,1)S(1)} collective-permute-done((bf16[112,384]{1,0:T(8,128)(2,1)S(1)}, bf16[112,384]{1,0:T(8,128)(2,1)S(1)}, u32[]{:S(2)}, u32[]{:S(2)}) %collective-permute-start) | collective-permute-done | bytes 86048 | tf_op jit(solution)/shard_map/ppermute | solution.py:127
  7.5 0.0 copy-start.4
  7.5 0.3 fusion
  7.8 0.0 copy-done.2
  7.8 0.3 copy-done.4
  8.2 0.1 slice_select_fusion.1
  8.3 19.0 %all_to_all.10 = f32[16,40,128]{2,1,0:T(8,128)S(1)} all-to-all(f32[16,40,128]{2,1,0:T(8,128)S(1)} %bitcast.9), channel_id=1, replica_groups=mesh['y'=8,'pair'=2,'side'=2,'expert'=8,'replica'=2] {'pair','y'}, dimensions={0} | all-to-all | bytes 655360 | tf_op jit(solution)/shard_map/all_to_all | solution.py:132
  27.3 0.0 copy-start
  27.4 17.1 %all_to_all.11 = f32[16,40,128]{2,1,0:T(8,128)} all-to-all(f32[16,40,128]{2,1,0:T(8,128)S(1)} %broadcast_in_dim.2), channel_id=1, replica_groups=mesh['y'=8,'pair'=2,'side'=2,'expert'=8,'replica'=2] {'pair','y'}, dimensions={0} | all-to-all | bytes 655360 | tf_op jit(solution)/shard_map/all_to_all | solution.py:134
  44.5 7.4 %shard_map.50 = (bf16[112,384]{1,0:T(8,128)(2,1)}, bf16[112,384]{1,0:T(8,128)(2,1)}) custom-call(f32[640,128]{1,0:T(8,128)} %bitcast.8, bf16[112,384]{1,0:T(8,128)(2,1)} %copy-done.2, bf16[112,384]{1,0:T(8,128)(2,1)} %copy-done.4), custom_call_target="tpu_custom_call" | custom-call | tf_op jit(solution)/shard_map/pallas_call | solution.py:136
  51.9 0.0 copy-start.5
  51.9 2.9 %collective-permute-start.1 = (bf16[112,384]{1,0:T(8,128)(2,1)}, bf16[112,384]{1,0:T(8,128)(2,1)S(1)}, u32[]{:S(2)}, u32[]{:S(2)}) collective-permute-start(bf16[112,384]{1,0:T(8,128)(2,1)} %get-tuple-element.9), channel_id=1, source_target_pairs={{0,16},{16,0},{1,17},{17,1},{2,18},{18,2},{3,19},{19,3},{4,20},{20... | collective-permute-start | bytes 258056 | tf_op jit(solution)/shard_map/ppermute | solution.py:141
  54.9 0.0 copy-done
  54.9 0.9 %convert_add_fusion = f32[4,112,384]{2,1,0:T(8,128)} fusion(bf16[4,112,384]{2,1,0:T(8,128)(2,1)S(1)} %copy-done.1, f32[4,112,384]{2,1,0:T(8,128)S(1)} %copy-done), kind=kLoop, calls=%fused_computation.1 | loop fusion | flops 516096 | bytes 1720320 | tf_op jit(solution)/shard_map/add | solution.py:129
  55.8 1.7 %collective-permute-done.1 = bf16[112,384]{1,0:T(8,128)(2,1)S(1)} collective-permute-done((bf16[112,384]{1,0:T(8,128)(2,1)}, bf16[112,384]{1,0:T(8,128)(2,1)S(1)}, u32[]{:S(2)}, u32[]{:S(2)}) %collective-permute-start.1) | collective-permute-done | bytes 86048 | tf_op jit(solution)/shard_map/ppermute | solution.py:141
  57.5 0.0 copy-done.5
  57.5 0.0 copy-start.3
  57.5 6.5 %all_gather.3 = bf16[4,112,384]{2,1,0:T(8,128)(2,1)S(1)} all-gather(bf16[2,112,384]{2,1,0:T(8,128)(2,1)S(1)} %maximum_select_fusion), channel_id=1, replica_groups=mesh['y'=8,'pair'=2,'side'=2,'expert'=8,'replica'=2] {'replica'}, dimensions={0}, use_global_device_ids=true | all-gather | bytes 516096 | tf_op jit(solution)/shard_map/all_gather | solution.py:143
  64.0 0.0 copy-done.3
  64.0 0.9 %add_convert_fusion = bf16[4,112,384]{2,1,0:T(8,128)(2,1)} fusion(bf16[4,112,384]{2,1,0:T(8,128)(2,1)S(1)} %copy-done.3, bf16[4,112,384]{2,1,0:T(8,128)(2,1)S(1)} %all_gather.3), kind=kLoop, calls=%fused_computation | loop fusion | flops 1032192 | bytes 1032192 | tf_op jit(solution)/shard_map/convert_element_type | solution.py:145
  (6 shorter events, 0.1 us)
Async XLA Ops:
  0.6 5.0 %copy-start.1 = (bf16[4,112,384]{2,1,0:T(8,128)(2,1)S(1)}, bf16[4,112,384]{2,1,0:T(8,128)(2,1)}, u32[]{:S(2)}) copy-start(bf16[4,112,384]{2,1,0:T(8,128)(2,1)} %param.4) | copy-start | bytes 1032196
  1.7 5.8 %collective-permute-start = (bf16[112,384]{1,0:T(8,128)(2,1)S(1)}, bf16[112,384]{1,0:T(8,128)(2,1)S(1)}, u32[]{:S(2)}, u32[]{:S(2)}) collective-permute-start(bf16[112,384]{1,0:T(8,128)(2,1)S(1)} %fusion.4), channel_id=1, source_target_pairs={{0,16},{16,0},{1,17},{17,1},{2,18},{18,2},{3,19},{19,3},{4,20},{20... | collective-permute-start | bytes 258056 | tf_op jit(solution)/shard_map/ppermute | solution.py:127
  6.6 1.2 %copy-start.2 = (bf16[112,384]{1,0:T(8,128)(2,1)}, bf16[112,384]{1,0:T(8,128)(2,1)S(1)}, u32[]{:S(2)}) copy-start(bf16[112,384]{1,0:T(8,128)(2,1)S(1)} %fusion.5.own_ref) | copy-start | bytes 258052
  7.5 0.6 copy-start.4
  27.3 27.5 %copy-start = (f32[4,112,384]{2,1,0:T(8,128)S(1)}, f32[4,112,384]{2,1,0:T(8,128)}, u32[]{:S(2)}) copy-start(f32[4,112,384]{2,1,0:T(8,128)} %param.3) | copy-start | bytes 2064388
  51.9 5.6 %copy-start.5 = (bf16[112,384]{1,0:T(8,128)(2,1)S(1)}, bf16[112,384]{1,0:T(8,128)(2,1)}, u32[]{:S(2)}) copy-start(bf16[112,384]{1,0:T(8,128)(2,1)} %get-tuple-element.8) | copy-start | bytes 258052
  51.9 5.6 %collective-permute-start.1 = (bf16[112,384]{1,0:T(8,128)(2,1)}, bf16[112,384]{1,0:T(8,128)(2,1)S(1)}, u32[]{:S(2)}, u32[]{:S(2)}) collective-permute-start(bf16[112,384]{1,0:T(8,128)(2,1)} %get-tuple-element.9), channel_id=1, source_target_pairs={{0,16},{16,0},{1,17},{17,1},{2,18},{18,2},{3,19},{19,3},{4,20},{20... | collective-permute-start | bytes 258056 | tf_op jit(solution)/shard_map/ppermute | solution.py:141
  57.5 6.5 %copy-start.3 = (bf16[4,112,384]{2,1,0:T(8,128)(2,1)S(1)}, bf16[4,112,384]{2,1,0:T(8,128)(2,1)}, u32[]{:S(2)}) copy-start(bf16[4,112,384]{2,1,0:T(8,128)(2,1)} %param.5) | copy-start | bytes 1032196

commit v5 on v4

--- a/solution.py
+++ b/solution.py
@@ -77,36 +77,24 @@
     return gram, jnp.sum(jnp.sum(trace, axis=1, keepdims=True), axis=0, keepdims=True)
 
 
-def chain_kernel(packed_ref, own_ref, got_ref, own_out_ref, got_out_ref, gram_ref, x_ref):
+def chain_kernel(packed_ref, own_ref, got_ref, own_out_ref, got_out_ref):
     count = own_ref.shape[0]
     gram, total = unpack(packed_ref)
     norm = jnp.sqrt(total) + NORM_EPS
-    gram_ref[...] = gram / (norm * norm)
-    x_ref[:count] = (own_ref[...].astype(f32) / norm).astype(bf16)
-    x_ref[count:] = (got_ref[...].astype(f32) / norm).astype(bf16)
-
-    def polynomial():
-        g = gram_ref[...].astype(bf16)
-        return (B_COEF * g.astype(f32) + C_COEF * dot(g, g)).astype(bf16)
-
-    def advance(poly):
-        iterate = x_ref[...]
-        return (A_COEF * iterate.astype(f32) + dot(iterate, poly)).astype(bf16)
-
-    def step(iteration, carry):
-        poly = polynomial()
-        gram = gram_ref[...]
+    gram = gram / (norm * norm)
+    rows = jnp.concatenate([own_ref[...], got_ref[...]], axis=0)
+    iterate = (rows.astype(f32) / norm).astype(bf16)
+    for iteration in range(ITERS):
+        last = iteration == ITERS - 1
         high, low = split(gram)
-        wide = jnp.concatenate([poly, poly], axis=1)
-        half = A_COEF * gram + dot(wide, jnp.concatenate([high, low], axis=0))
-        high, low = split(half)
-        tall = jnp.concatenate([poly, poly], axis=0)
-        gram_ref[...] = A_COEF * half + dot(jnp.concatenate([high, low], axis=1), tall)
-        x_ref[...] = advance(poly)
-        return carry
-
-    lax.fori_loop(0, ITERS - 1, step, 0)
-    iterate = advance(polynomial())
+        poly = (B_COEF * high.astype(f32) + C_COEF * dot(high, high)).astype(bf16)
+        if not last:
+            wide = jnp.concatenate([poly, poly], axis=1)
+            half = A_COEF * gram + dot(wide, jnp.concatenate([high, low], axis=0))
+        iterate = (A_COEF * iterate.astype(f32) + dot(iterate, poly)).astype(bf16)
+        if not last:
+            tall = jnp.concatenate([poly, poly], axis=0)
+            gram = A_COEF * half + dot(jnp.concatenate(split(half), axis=1), tall)
     own_out_ref[...] = iterate[:count]
     got_out_ref[...] = iterate[count:]
 
@@ -136,7 +124,6 @@
     own, got = pl.pallas_call(
         chain_kernel,
         out_shape=(piece, piece),
-        scratch_shapes=[pltpu.VMEM((C, C), f32), pltpu.VMEM((2 * rows, C), bf16)],
     )(packed.reshape(partial.shape), own, got)
     got = lax.ppermute(got, "side", [(0, 1), (1, 0)])
     both = jnp.where(side == 0, jnp.stack([own, got]), jnp.stack([got, own]))

time: 65.2 us -> 64.7 us (level)
  no operation moved by 1% of the time
where the time goes in v5:
time: 64.7 us; the launch traced here: 64.4 us
  blocking collectives  42.6 us (66%)
  Pallas kernels  6.9 us (11%)
  starting transfers between devices  6.88 us (11%)
  other arithmetic  3.97 us (6%)
  waiting for transfers between devices  2.55 us (4%)
  between operations  0.78 us (1%)
    all_to_all x1, blocking collectives, body(): lax.all_to_all(pieces, ('pair', 'y'), split_axis=0, concat_axis=0, tiled=...  19 us
    all_to_all x1, blocking collectives, body(): lax.all_to_all(total, ('pair', 'y'), split_axis=0, concat_axis=0, tiled=T...  17.1 us
    pallas_call x1, Pallas kernels, body(): pl.pallas_call(chain_kernel, out_shape=(piece, piece))  6.9 us
    all_gather x1, blocking collectives, body(): finished = lax.all_gather(both, 'replica', axis=0, tiled=True)  6.47 us
    ppermute x1, starting transfers between devices, body(): got = lax.ppermute(sent, 'side', [(0, 1), (1, 0)])  3.95 us
    ppermute x1, starting transfers between devices, body(): got = lax.ppermute(got, 'side', [(0, 1), (1, 0)])  2.94 us
    convert_element_type x2, other arithmetic, rounded(): return (MOMENTUM_COEF * m + g.astype(f32)).astype(bf16)  1.99 us
    ppermute x1, waiting for transfers between devices, body(): got = lax.ppermute(got, 'side', [(0, 1), (1, 0)])  1.68 us
  transfers between devices with their start and end apart: 2, of which 2 were waited for; matrix products, arithmetic and copies ran while one was open for 3% of the time, Pallas kernels for 0%

profile of v5, /device:TPU:1, one launch (start us, length us, event | category | flops | bytes accessed | tf_op | source)
XLA Modules:
  0.0 64.4 jit_solution(11546522270581270041)
XLA Ops:
  0.6 0.0 copy-start.1
  0.7 1.0 %fusion.4 = bf16[112,384]{1,0:T(8,128)(2,1)S(1)} fusion(f32[4,112,384]{2,1,0:T(8,128)} %param.3, s32[]{:T(128)S(6)} %select_n.29, bf16[4,112,384]{2,1,0:T(8,128)(2,1)} %param.4), kind=kLoop, calls=%fused_computation.10 | loop fusion | flops 172032 | bytes 344068 | tf_op jit(solution)/shard_map/convert_element_type | solution.py:111
  1.7 3.9 %collective-permute-start = (bf16[112,384]{1,0:T(8,128)(2,1)S(1)}, bf16[112,384]{1,0:T(8,128)(2,1)S(1)}, u32[]{:S(2)}, u32[]{:S(2)}) collective-permute-start(bf16[112,384]{1,0:T(8,128)(2,1)S(1)} %fusion.4), channel_id=1, source_target_pairs={{0,16},{16,0},{1,17},{17,1},{2,18},{18,2},{3,19},{19,3},{4,20},{20... | collective-permute-start | bytes 258056 | tf_op jit(solution)/shard_map/ppermute | solution.py:115
  5.7 0.0 copy-done.1
  5.7 1.0 %fusion.5.own_ref = bf16[112,384]{1,0:T(8,128)(2,1)S(1)} fusion(f32[4,112,384]{2,1,0:T(8,128)} %param.3, s32[]{:T(128)S(6)} %select_n.30, bf16[4,112,384]{2,1,0:T(8,128)(2,1)S(1)} %copy-done.1), kind=kLoop, calls=%fused_computation.11 | loop fusion | flops 172032 | bytes 344068 | tf_op jit(solution)/shard_map/convert_element_type | solution.py:111
  6.6 0.0 copy-start.2
  6.6 0.9 %collective-permute-done.got_ref = bf16[112,384]{1,0:T(8,128)(2,1)S(1)} collective-permute-done((bf16[112,384]{1,0:T(8,128)(2,1)S(1)}, bf16[112,384]{1,0:T(8,128)(2,1)S(1)}, u32[]{:S(2)}, u32[]{:S(2)}) %collective-permute-start) | collective-permute-done | bytes 86048 | tf_op jit(solution)/shard_map/ppermute | solution.py:115
  7.5 0.0 copy-start.4
  7.5 0.3 fusion
  7.8 0.0 copy-done.2
  7.8 0.3 copy-done.4
  8.2 0.1 slice_select_fusion.1
  8.3 19.0 %all_to_all.10 = f32[16,40,128]{2,1,0:T(8,128)S(1)} all-to-all(f32[16,40,128]{2,1,0:T(8,128)S(1)} %bitcast.9), channel_id=1, replica_groups=mesh['y'=8,'pair'=2,'side'=2,'expert'=8,'replica'=2] {'pair','y'}, dimensions={0} | all-to-all | bytes 655360 | tf_op jit(solution)/shard_map/all_to_all | solution.py:120
  27.3 0.0 copy-start
  27.4 17.1 %all_to_all.11 = f32[16,40,128]{2,1,0:T(8,128)} all-to-all(f32[16,40,128]{2,1,0:T(8,128)S(1)} %broadcast_in_dim.2), channel_id=1, replica_groups=mesh['y'=8,'pair'=2,'side'=2,'expert'=8,'replica'=2] {'pair','y'}, dimensions={0} | all-to-all | bytes 655360 | tf_op jit(solution)/shard_map/all_to_all | solution.py:122
  44.5 6.9 %shard_map.50 = (bf16[112,384]{1,0:T(8,128)(2,1)}, bf16[112,384]{1,0:T(8,128)(2,1)}) custom-call(f32[640,128]{1,0:T(8,128)} %bitcast.8, bf16[112,384]{1,0:T(8,128)(2,1)} %copy-done.2, bf16[112,384]{1,0:T(8,128)(2,1)} %copy-done.4), custom_call_target="tpu_custom_call" | custom-call | tf_op jit(solution)/shard_map/pallas_call | solution.py:124
  51.4 0.0 copy-start.5
  51.4 2.9 %collective-permute-start.1 = (bf16[112,384]{1,0:T(8,128)(2,1)}, bf16[112,384]{1,0:T(8,128)(2,1)S(1)}, u32[]{:S(2)}, u32[]{:S(2)}) collective-permute-start(bf16[112,384]{1,0:T(8,128)(2,1)} %get-tuple-element.9), channel_id=1, source_target_pairs={{0,16},{16,0},{1,17},{17,1},{2,18},{18,2},{3,19},{19,3},{4,20},{20... | collective-permute-start | bytes 258056 | tf_op jit(solution)/shard_map/ppermute | solution.py:128
  54.4 0.0 copy-done
  54.4 0.9 %convert_add_fusion = f32[4,112,384]{2,1,0:T(8,128)} fusion(bf16[4,112,384]{2,1,0:T(8,128)(2,1)S(1)} %copy-done.1, f32[4,112,384]{2,1,0:T(8,128)S(1)} %copy-done), kind=kLoop, calls=%fused_computation.1 | loop fusion | flops 516096 | bytes 1720320 | tf_op jit(solution)/shard_map/add | solution.py:117
  55.3 1.7 %collective-permute-done.1 = bf16[112,384]{1,0:T(8,128)(2,1)S(1)} collective-permute-done((bf16[112,384]{1,0:T(8,128)(2,1)}, bf16[112,384]{1,0:T(8,128)(2,1)S(1)}, u32[]{:S(2)}, u32[]{:S(2)}) %collective-permute-start.1) | collective-permute-done | bytes 86048 | tf_op jit(solution)/shard_map/ppermute | solution.py:128
  57.0 0.0 copy-done.5
  57.0 0.0 copy-start.3
  57.0 6.5 %all_gather.3 = bf16[4,112,384]{2,1,0:T(8,128)(2,1)S(1)} all-gather(bf16[2,112,384]{2,1,0:T(8,128)(2,1)S(1)} %maximum_select_fusion), channel_id=1, replica_groups=mesh['y'=8,'pair'=2,'side'=2,'expert'=8,'replica'=2] {'replica'}, dimensions={0}, use_global_device_ids=true | all-gather | bytes 516096 | tf_op jit(solution)/shard_map/all_gather | solution.py:130
  63.5 0.0 copy-done.3
  63.5 0.9 %add_convert_fusion = bf16[4,112,384]{2,1,0:T(8,128)(2,1)} fusion(bf16[4,112,384]{2,1,0:T(8,128)(2,1)S(1)} %copy-done.3, bf16[4,112,384]{2,1,0:T(8,128)(2,1)S(1)} %all_gather.3), kind=kLoop, calls=%fused_computation | loop fusion | flops 1032192 | bytes 1032192 | tf_op jit(solution)/shard_map/convert_element_type | solution.py:132
  (6 shorter events, 0.1 us)
Async XLA Ops:
  0.6 5.0 %copy-start.1 = (bf16[4,112,384]{2,1,0:T(8,128)(2,1)S(1)}, bf16[4,112,384]{2,1,0:T(8,128)(2,1)}, u32[]{:S(2)}) copy-start(bf16[4,112,384]{2,1,0:T(8,128)(2,1)} %param.4) | copy-start | bytes 1032196
  1.7 5.8 %collective-permute-start = (bf16[112,384]{1,0:T(8,128)(2,1)S(1)}, bf16[112,384]{1,0:T(8,128)(2,1)S(1)}, u32[]{:S(2)}, u32[]{:S(2)}) collective-permute-start(bf16[112,384]{1,0:T(8,128)(2,1)S(1)} %fusion.4), channel_id=1, source_target_pairs={{0,16},{16,0},{1,17},{17,1},{2,18},{18,2},{3,19},{19,3},{4,20},{20... | collective-permute-start | bytes 258056 | tf_op jit(solution)/shard_map/ppermute | solution.py:115
  6.6 1.2 %copy-start.2 = (bf16[112,384]{1,0:T(8,128)(2,1)}, bf16[112,384]{1,0:T(8,128)(2,1)S(1)}, u32[]{:S(2)}) copy-start(bf16[112,384]{1,0:T(8,128)(2,1)S(1)} %fusion.5.own_ref) | copy-start | bytes 258052
  7.5 0.6 copy-start.4
  27.3 27.0 %copy-start = (f32[4,112,384]{2,1,0:T(8,128)S(1)}, f32[4,112,384]{2,1,0:T(8,128)}, u32[]{:S(2)}) copy-start(f32[4,112,384]{2,1,0:T(8,128)} %param.3) | copy-start | bytes 2064388
  51.4 5.6 %copy-start.5 = (bf16[112,384]{1,0:T(8,128)(2,1)S(1)}, bf16[112,384]{1,0:T(8,128)(2,1)}, u32[]{:S(2)}) copy-start(bf16[112,384]{1,0:T(8,128)(2,1)} %get-tuple-element.8) | copy-start | bytes 258052
  51.4 5.6 %collective-permute-start.1 = (bf16[112,384]{1,0:T(8,128)(2,1)}, bf16[112,384]{1,0:T(8,128)(2,1)S(1)}, u32[]{:S(2)}, u32[]{:S(2)}) collective-permute-start(bf16[112,384]{1,0:T(8,128)(2,1)} %get-tuple-element.9), channel_id=1, source_target_pairs={{0,16},{16,0},{1,17},{17,1},{2,18},{18,2},{3,19},{19,3},{4,20},{20... | collective-permute-start | bytes 258056 | tf_op jit(solution)/shard_map/ppermute | solution.py:128
  57.0 6.5 %copy-start.3 = (bf16[4,112,384]{2,1,0:T(8,128)(2,1)S(1)}, bf16[4,112,384]{2,1,0:T(8,128)(2,1)}, u32[]{:S(2)}) copy-start(bf16[4,112,384]{2,1,0:T(8,128)(2,1)} %param.5) | copy-start | bytes 1032196

commit v6 on v5

--- a/solution.py
+++ b/solution.py
@@ -78,25 +78,32 @@
 
 
 def chain_kernel(packed_ref, own_ref, got_ref, own_out_ref, got_out_ref):
-    count = own_ref.shape[0]
     gram, total = unpack(packed_ref)
     norm = jnp.sqrt(total) + NORM_EPS
     gram = gram / (norm * norm)
-    rows = jnp.concatenate([own_ref[...], got_ref[...]], axis=0)
-    iterate = (rows.astype(f32) / norm).astype(bf16)
+    own = (own_ref[...].astype(f32) / norm).astype(bf16)
+    got = (got_ref[...].astype(f32) / norm).astype(bf16)
+
+    def advance(rows, poly):
+        return (A_COEF * rows.astype(f32) + dot(rows, poly)).astype(bf16)
+
+    poly = None
     for iteration in range(ITERS):
         last = iteration == ITERS - 1
         high, low = split(gram)
-        poly = (B_COEF * high.astype(f32) + C_COEF * dot(high, high)).astype(bf16)
+        square = dot(high, high)
+        if iteration > 0:
+            own = advance(own, poly)
+        poly = (B_COEF * high.astype(f32) + C_COEF * square).astype(bf16)
         if not last:
             wide = jnp.concatenate([poly, poly], axis=1)
             half = A_COEF * gram + dot(wide, jnp.concatenate([high, low], axis=0))
-        iterate = (A_COEF * iterate.astype(f32) + dot(iterate, poly)).astype(bf16)
+        got = advance(got, poly)
         if not last:
             tall = jnp.concatenate([poly, poly], axis=0)
             gram = A_COEF * half + dot(jnp.concatenate(split(half), axis=1), tall)
-    own_out_ref[...] = iterate[:count]
-    got_out_ref[...] = iterate[count:]
+    own_out_ref[...] = advance(own, poly)
+    got_out_ref[...] = got
 
 
 def body(momentum, gradient, weight):

time: 64.7 us -> 64.4 us (level)
  no operation moved by 1% of the time
where the time goes in v6:
time: 64.4 us; the launch traced here: 64.1 us
  blocking collectives  42.6 us (66%)
  starting transfers between devices  6.89 us (11%)
  Pallas kernels  6.61 us (10%)
  other arithmetic  3.97 us (6%)
  waiting for transfers between devices  2.54 us (4%)
  between operations  0.78 us (1%)
    all_to_all x1, blocking collectives, body(): lax.all_to_all(pieces, ('pair', 'y'), split_axis=0, concat_axis=0, tiled=...  19 us
    all_to_all x1, blocking collectives, body(): lax.all_to_all(total, ('pair', 'y'), split_axis=0, concat_axis=0, tiled=T...  17.1 us
    pallas_call x1, Pallas kernels, body(): pl.pallas_call(chain_kernel, out_shape=(piece, piece))  6.61 us
    all_gather x1, blocking collectives, body(): finished = lax.all_gather(both, 'replica', axis=0, tiled=True)  6.47 us
    ppermute x1, starting transfers between devices, body(): got = lax.ppermute(sent, 'side', [(0, 1), (1, 0)])  3.95 us
    ppermute x1, starting transfers between devices, body(): got = lax.ppermute(got, 'side', [(0, 1), (1, 0)])  2.94 us
    convert_element_type x2, other arithmetic, rounded(): return (MOMENTUM_COEF * m + g.astype(f32)).astype(bf16)  1.99 us
    ppermute x1, waiting for transfers between devices, body(): got = lax.ppermute(got, 'side', [(0, 1), (1, 0)])  1.68 us
  transfers between devices with their start and end apart: 2, of which 2 were waited for; matrix products, arithmetic and copies ran while one was open for 3% of the time, Pallas kernels for 0%

profile of v6, /device:TPU:1, one launch (start us, length us, event | category | flops | bytes accessed | tf_op | source)
XLA Modules:
  0.0 64.1 jit_solution(9479927684879948182)
XLA Ops:
  0.6 0.0 copy-start.1
  0.7 1.0 %fusion.4 = bf16[112,384]{1,0:T(8,128)(2,1)S(1)} fusion(f32[4,112,384]{2,1,0:T(8,128)} %param.3, s32[]{:T(128)S(6)} %select_n.29, bf16[4,112,384]{2,1,0:T(8,128)(2,1)} %param.4), kind=kLoop, calls=%fused_computation.10 | loop fusion | flops 172032 | bytes 344068 | tf_op jit(solution)/shard_map/convert_element_type | solution.py:118
  1.7 3.9 %collective-permute-start = (bf16[112,384]{1,0:T(8,128)(2,1)S(1)}, bf16[112,384]{1,0:T(8,128)(2,1)S(1)}, u32[]{:S(2)}, u32[]{:S(2)}) collective-permute-start(bf16[112,384]{1,0:T(8,128)(2,1)S(1)} %fusion.4), channel_id=1, source_target_pairs={{0,16},{16,0},{1,17},{17,1},{2,18},{18,2},{3,19},{19,3},{4,20},{20... | collective-permute-start | bytes 258056 | tf_op jit(solution)/shard_map/ppermute | solution.py:122
  5.7 0.0 copy-done.1
  5.7 1.0 %fusion.5.own_ref = bf16[112,384]{1,0:T(8,128)(2,1)S(1)} fusion(f32[4,112,384]{2,1,0:T(8,128)} %param.3, s32[]{:T(128)S(6)} %select_n.30, bf16[4,112,384]{2,1,0:T(8,128)(2,1)S(1)} %copy-done.1), kind=kLoop, calls=%fused_computation.11 | loop fusion | flops 172032 | bytes 344068 | tf_op jit(solution)/shard_map/convert_element_type | solution.py:118
  6.6 0.0 copy-start.2
  6.6 0.9 %collective-permute-done.got_ref = bf16[112,384]{1,0:T(8,128)(2,1)S(1)} collective-permute-done((bf16[112,384]{1,0:T(8,128)(2,1)S(1)}, bf16[112,384]{1,0:T(8,128)(2,1)S(1)}, u32[]{:S(2)}, u32[]{:S(2)}) %collective-permute-start) | collective-permute-done | bytes 86048 | tf_op jit(solution)/shard_map/ppermute | solution.py:122
  7.5 0.0 copy-start.4
  7.5 0.3 fusion
  7.8 0.0 copy-done.2
  7.8 0.3 copy-done.4
  8.2 0.1 slice_select_fusion.1
  8.3 19.0 %all_to_all.10 = f32[16,40,128]{2,1,0:T(8,128)S(1)} all-to-all(f32[16,40,128]{2,1,0:T(8,128)S(1)} %bitcast.9), channel_id=1, replica_groups=mesh['y'=8,'pair'=2,'side'=2,'expert'=8,'replica'=2] {'pair','y'}, dimensions={0} | all-to-all | bytes 655360 | tf_op jit(solution)/shard_map/all_to_all | solution.py:127
  27.3 0.0 copy-start
  27.4 17.1 %all_to_all.11 = f32[16,40,128]{2,1,0:T(8,128)} all-to-all(f32[16,40,128]{2,1,0:T(8,128)S(1)} %broadcast_in_dim.2), channel_id=1, replica_groups=mesh['y'=8,'pair'=2,'side'=2,'expert'=8,'replica'=2] {'pair','y'}, dimensions={0} | all-to-all | bytes 655360 | tf_op jit(solution)/shard_map/all_to_all | solution.py:129
  44.5 6.6 %shard_map.50 = (bf16[112,384]{1,0:T(8,128)(2,1)}, bf16[112,384]{1,0:T(8,128)(2,1)}) custom-call(f32[640,128]{1,0:T(8,128)} %bitcast.8, bf16[112,384]{1,0:T(8,128)(2,1)} %copy-done.2, bf16[112,384]{1,0:T(8,128)(2,1)} %copy-done.4), custom_call_target="tpu_custom_call" | custom-call | tf_op jit(solution)/shard_map/pallas_call | solution.py:131
  51.1 0.0 copy-start.5
  51.1 2.9 %collective-permute-start.1 = (bf16[112,384]{1,0:T(8,128)(2,1)}, bf16[112,384]{1,0:T(8,128)(2,1)S(1)}, u32[]{:S(2)}, u32[]{:S(2)}) collective-permute-start(bf16[112,384]{1,0:T(8,128)(2,1)} %get-tuple-element.9), channel_id=1, source_target_pairs={{0,16},{16,0},{1,17},{17,1},{2,18},{18,2},{3,19},{19,3},{4,20},{20... | collective-permute-start | bytes 258056 | tf_op jit(solution)/shard_map/ppermute | solution.py:135
  54.1 0.0 copy-done
  54.1 0.9 %convert_add_fusion = f32[4,112,384]{2,1,0:T(8,128)} fusion(bf16[4,112,384]{2,1,0:T(8,128)(2,1)S(1)} %copy-done.1, f32[4,112,384]{2,1,0:T(8,128)S(1)} %copy-done), kind=kLoop, calls=%fused_computation.1 | loop fusion | flops 516096 | bytes 1720320 | tf_op jit(solution)/shard_map/add | solution.py:124
  55.0 1.7 %collective-permute-done.1 = bf16[112,384]{1,0:T(8,128)(2,1)S(1)} collective-permute-done((bf16[112,384]{1,0:T(8,128)(2,1)}, bf16[112,384]{1,0:T(8,128)(2,1)S(1)}, u32[]{:S(2)}, u32[]{:S(2)}) %collective-permute-start.1) | collective-permute-done | bytes 86048 | tf_op jit(solution)/shard_map/ppermute | solution.py:135
  56.7 0.0 copy-done.5
  56.7 0.0 copy-start.3
  56.7 6.5 %all_gather.3 = bf16[4,112,384]{2,1,0:T(8,128)(2,1)S(1)} all-gather(bf16[2,112,384]{2,1,0:T(8,128)(2,1)S(1)} %maximum_select_fusion), channel_id=1, replica_groups=mesh['y'=8,'pair'=2,'side'=2,'expert'=8,'replica'=2] {'replica'}, dimensions={0}, use_global_device_ids=true | all-gather | bytes 516096 | tf_op jit(solution)/shard_map/all_gather | solution.py:137
  63.2 0.0 copy-done.3
  63.2 0.9 %add_convert_fusion = bf16[4,112,384]{2,1,0:T(8,128)(2,1)} fusion(bf16[4,112,384]{2,1,0:T(8,128)(2,1)S(1)} %copy-done.3, bf16[4,112,384]{2,1,0:T(8,128)(2,1)S(1)} %all_gather.3), kind=kLoop, calls=%fused_computation | loop fusion | flops 1032192 | bytes 1032192 | tf_op jit(solution)/shard_map/convert_element_type | solution.py:139
  (6 shorter events, 0.1 us)
Async XLA Ops:
  0.6 5.0 %copy-start.1 = (bf16[4,112,384]{2,1,0:T(8,128)(2,1)S(1)}, bf16[4,112,384]{2,1,0:T(8,128)(2,1)}, u32[]{:S(2)}) copy-start(bf16[4,112,384]{2,1,0:T(8,128)(2,1)} %param.4) | copy-start | bytes 1032196
  1.7 5.8 %collective-permute-start = (bf16[112,384]{1,0:T(8,128)(2,1)S(1)}, bf16[112,384]{1,0:T(8,128)(2,1)S(1)}, u32[]{:S(2)}, u32[]{:S(2)}) collective-permute-start(bf16[112,384]{1,0:T(8,128)(2,1)S(1)} %fusion.4), channel_id=1, source_target_pairs={{0,16},{16,0},{1,17},{17,1},{2,18},{18,2},{3,19},{19,3},{4,20},{20... | collective-permute-start | bytes 258056 | tf_op jit(solution)/shard_map/ppermute | solution.py:122
  6.6 1.2 %copy-start.2 = (bf16[112,384]{1,0:T(8,128)(2,1)}, bf16[112,384]{1,0:T(8,128)(2,1)S(1)}, u32[]{:S(2)}) copy-start(bf16[112,384]{1,0:T(8,128)(2,1)S(1)} %fusion.5.own_ref) | copy-start | bytes 258052
  7.5 0.6 copy-start.4
  27.3 26.8 %copy-start = (f32[4,112,384]{2,1,0:T(8,128)S(1)}, f32[4,112,384]{2,1,0:T(8,128)}, u32[]{:S(2)}) copy-start(f32[4,112,384]{2,1,0:T(8,128)} %param.3) | copy-start | bytes 2064388
  51.1 5.6 %copy-start.5 = (bf16[112,384]{1,0:T(8,128)(2,1)S(1)}, bf16[112,384]{1,0:T(8,128)(2,1)}, u32[]{:S(2)}) copy-start(bf16[112,384]{1,0:T(8,128)(2,1)} %get-tuple-element.8) | copy-start | bytes 258052
  51.1 5.6 %collective-permute-start.1 = (bf16[112,384]{1,0:T(8,128)(2,1)}, bf16[112,384]{1,0:T(8,128)(2,1)S(1)}, u32[]{:S(2)}, u32[]{:S(2)}) collective-permute-start(bf16[112,384]{1,0:T(8,128)(2,1)} %get-tuple-element.9), channel_id=1, source_target_pairs={{0,16},{16,0},{1,17},{17,1},{2,18},{18,2},{3,19},{19,3},{4,20},{20... | collective-permute-start | bytes 258056 | tf_op jit(solution)/shard_map/ppermute | solution.py:135
  56.7 6.5 %copy-start.3 = (bf16[4,112,384]{2,1,0:T(8,128)(2,1)S(1)}, bf16[4,112,384]{2,1,0:T(8,128)(2,1)}, u32[]{:S(2)}) copy-start(bf16[4,112,384]{2,1,0:T(8,128)(2,1)} %param.5) | copy-start | bytes 1032196

commit v7 on v6

--- a/solution.py
+++ b/solution.py
@@ -80,9 +80,7 @@
 def chain_kernel(packed_ref, own_ref, got_ref, own_out_ref, got_out_ref):
     gram, total = unpack(packed_ref)
     norm = jnp.sqrt(total) + NORM_EPS
-    gram = gram / (norm * norm)
-    own = (own_ref[...].astype(f32) / norm).astype(bf16)
-    got = (got_ref[...].astype(f32) / norm).astype(bf16)
+    gram = gram * (1.0 / (norm * norm))
 
     def advance(rows, poly):
         return (A_COEF * rows.astype(f32) + dot(rows, poly)).astype(bf16)
@@ -92,7 +90,10 @@
         last = iteration == ITERS - 1
         high, low = split(gram)
         square = dot(high, high)
-        if iteration > 0:
+        if iteration == 0:
+            own = (own_ref[...].astype(f32) / norm).astype(bf16)
+            got = (got_ref[...].astype(f32) / norm).astype(bf16)
+        else:
             own = advance(own, poly)
         poly = (B_COEF * high.astype(f32) + C_COEF * square).astype(bf16)
         if not last:

time: 64.4 us -> 64.4 us (level)
  no operation moved by 1% of the time
where the time goes in v7:
time: 64.4 us; the launch traced here: 64.1 us
  blocking collectives  42.6 us (66%)
  starting transfers between devices  6.89 us (11%)
  Pallas kernels  6.61 us (10%)
  other arithmetic  3.97 us (6%)
  waiting for transfers between devices  2.54 us (4%)
  between operations  0.78 us (1%)
    all_to_all x1, blocking collectives, body(): lax.all_to_all(pieces, ('pair', 'y'), split_axis=0, concat_axis=0, tiled=...  19 us
    all_to_all x1, blocking collectives, body(): lax.all_to_all(total, ('pair', 'y'), split_axis=0, concat_axis=0, tiled=T...  17.1 us
    pallas_call x1, Pallas kernels, body(): pl.pallas_call(chain_kernel, out_shape=(piece, piece))  6.61 us
    all_gather x1, blocking collectives, body(): finished = lax.all_gather(both, 'replica', axis=0, tiled=True)  6.47 us
    ppermute x1, starting transfers between devices, body(): got = lax.ppermute(sent, 'side', [(0, 1), (1, 0)])  3.95 us
    ppermute x1, starting transfers between devices, body(): got = lax.ppermute(got, 'side', [(0, 1), (1, 0)])  2.94 us
    convert_element_type x2, other arithmetic, rounded(): return (MOMENTUM_COEF * m + g.astype(f32)).astype(bf16)  1.99 us
    ppermute x1, waiting for transfers between devices, body(): got = lax.ppermute(got, 'side', [(0, 1), (1, 0)])  1.68 us
  transfers between devices with their start and end apart: 2, of which 2 were waited for; matrix products, arithmetic and copies ran while one was open for 3% of the time, Pallas kernels for 0%

profile of v7, /device:TPU:1, one launch (start us, length us, event | category | flops | bytes accessed | tf_op | source)
XLA Modules:
  0.0 64.1 jit_solution(9479927684879948182)
XLA Ops:
  0.6 0.0 copy-start.1
  0.7 1.0 %fusion.4 = bf16[112,384]{1,0:T(8,128)(2,1)S(1)} fusion(f32[4,112,384]{2,1,0:T(8,128)} %param.3, s32[]{:T(128)S(6)} %select_n.29, bf16[4,112,384]{2,1,0:T(8,128)(2,1)} %param.4), kind=kLoop, calls=%fused_computation.10 | loop fusion | flops 172032 | bytes 344068 | tf_op jit(solution)/shard_map/convert_element_type | solution.py:119
  1.7 3.9 %collective-permute-start = (bf16[112,384]{1,0:T(8,128)(2,1)S(1)}, bf16[112,384]{1,0:T(8,128)(2,1)S(1)}, u32[]{:S(2)}, u32[]{:S(2)}) collective-permute-start(bf16[112,384]{1,0:T(8,128)(2,1)S(1)} %fusion.4), channel_id=1, source_target_pairs={{0,16},{16,0},{1,17},{17,1},{2,18},{18,2},{3,19},{19,3},{4,20},{20... | collective-permute-start | bytes 258056 | tf_op jit(solution)/shard_map/ppermute | solution.py:123
  5.7 0.0 copy-done.1
  5.7 1.0 %fusion.5.own_ref = bf16[112,384]{1,0:T(8,128)(2,1)S(1)} fusion(f32[4,112,384]{2,1,0:T(8,128)} %param.3, s32[]{:T(128)S(6)} %select_n.30, bf16[4,112,384]{2,1,0:T(8,128)(2,1)S(1)} %copy-done.1), kind=kLoop, calls=%fused_computation.11 | loop fusion | flops 172032 | bytes 344068 | tf_op jit(solution)/shard_map/convert_element_type | solution.py:119
  6.6 0.0 copy-start.2
  6.6 0.9 %collective-permute-done.got_ref = bf16[112,384]{1,0:T(8,128)(2,1)S(1)} collective-permute-done((bf16[112,384]{1,0:T(8,128)(2,1)S(1)}, bf16[112,384]{1,0:T(8,128)(2,1)S(1)}, u32[]{:S(2)}, u32[]{:S(2)}) %collective-permute-start) | collective-permute-done | bytes 86048 | tf_op jit(solution)/shard_map/ppermute | solution.py:123
  7.5 0.0 copy-start.4
  7.5 0.3 fusion
  7.8 0.0 copy-done.2
  7.8 0.3 copy-done.4
  8.2 0.1 slice_select_fusion.1
  8.3 19.0 %all_to_all.10 = f32[16,40,128]{2,1,0:T(8,128)S(1)} all-to-all(f32[16,40,128]{2,1,0:T(8,128)S(1)} %bitcast.9), channel_id=1, replica_groups=mesh['y'=8,'pair'=2,'side'=2,'expert'=8,'replica'=2] {'pair','y'}, dimensions={0} | all-to-all | bytes 655360 | tf_op jit(solution)/shard_map/all_to_all | solution.py:128
  27.3 0.0 copy-start
  27.4 17.1 %all_to_all.11 = f32[16,40,128]{2,1,0:T(8,128)} all-to-all(f32[16,40,128]{2,1,0:T(8,128)S(1)} %broadcast_in_dim.2), channel_id=1, replica_groups=mesh['y'=8,'pair'=2,'side'=2,'expert'=8,'replica'=2] {'pair','y'}, dimensions={0} | all-to-all | bytes 655360 | tf_op jit(solution)/shard_map/all_to_all | solution.py:130
  44.5 6.6 %shard_map.50 = (bf16[112,384]{1,0:T(8,128)(2,1)}, bf16[112,384]{1,0:T(8,128)(2,1)}) custom-call(f32[640,128]{1,0:T(8,128)} %bitcast.8, bf16[112,384]{1,0:T(8,128)(2,1)} %copy-done.2, bf16[112,384]{1,0:T(8,128)(2,1)} %copy-done.4), custom_call_target="tpu_custom_call" | custom-call | tf_op jit(solution)/shard_map/pallas_call | solution.py:132
  51.1 0.0 copy-start.5
  51.1 2.9 %collective-permute-start.1 = (bf16[112,384]{1,0:T(8,128)(2,1)}, bf16[112,384]{1,0:T(8,128)(2,1)S(1)}, u32[]{:S(2)}, u32[]{:S(2)}) collective-permute-start(bf16[112,384]{1,0:T(8,128)(2,1)} %get-tuple-element.9), channel_id=1, source_target_pairs={{0,16},{16,0},{1,17},{17,1},{2,18},{18,2},{3,19},{19,3},{4,20},{20... | collective-permute-start | bytes 258056 | tf_op jit(solution)/shard_map/ppermute | solution.py:136
  54.1 0.0 copy-done
  54.1 0.9 %convert_add_fusion = f32[4,112,384]{2,1,0:T(8,128)} fusion(bf16[4,112,384]{2,1,0:T(8,128)(2,1)S(1)} %copy-done.1, f32[4,112,384]{2,1,0:T(8,128)S(1)} %copy-done), kind=kLoop, calls=%fused_computation.1 | loop fusion | flops 516096 | bytes 1720320 | tf_op jit(solution)/shard_map/add | solution.py:125
  55.0 1.7 %collective-permute-done.1 = bf16[112,384]{1,0:T(8,128)(2,1)S(1)} collective-permute-done((bf16[112,384]{1,0:T(8,128)(2,1)}, bf16[112,384]{1,0:T(8,128)(2,1)S(1)}, u32[]{:S(2)}, u32[]{:S(2)}) %collective-permute-start.1) | collective-permute-done | bytes 86048 | tf_op jit(solution)/shard_map/ppermute | solution.py:136
  56.7 0.0 copy-done.5
  56.7 0.0 copy-start.3
  56.7 6.5 %all_gather.3 = bf16[4,112,384]{2,1,0:T(8,128)(2,1)S(1)} all-gather(bf16[2,112,384]{2,1,0:T(8,128)(2,1)S(1)} %maximum_select_fusion), channel_id=1, replica_groups=mesh['y'=8,'pair'=2,'side'=2,'expert'=8,'replica'=2] {'replica'}, dimensions={0}, use_global_device_ids=true | all-gather | bytes 516096 | tf_op jit(solution)/shard_map/all_gather | solution.py:138
  63.2 0.0 copy-done.3
  63.2 0.9 %add_convert_fusion = bf16[4,112,384]{2,1,0:T(8,128)(2,1)} fusion(bf16[4,112,384]{2,1,0:T(8,128)(2,1)S(1)} %copy-done.3, bf16[4,112,384]{2,1,0:T(8,128)(2,1)S(1)} %all_gather.3), kind=kLoop, calls=%fused_computation | loop fusion | flops 1032192 | bytes 1032192 | tf_op jit(solution)/shard_map/convert_element_type | solution.py:140
  (6 shorter events, 0.1 us)
Async XLA Ops:
  0.6 5.0 %copy-start.1 = (bf16[4,112,384]{2,1,0:T(8,128)(2,1)S(1)}, bf16[4,112,384]{2,1,0:T(8,128)(2,1)}, u32[]{:S(2)}) copy-start(bf16[4,112,384]{2,1,0:T(8,128)(2,1)} %param.4) | copy-start | bytes 1032196
  1.7 5.8 %collective-permute-start = (bf16[112,384]{1,0:T(8,128)(2,1)S(1)}, bf16[112,384]{1,0:T(8,128)(2,1)S(1)}, u32[]{:S(2)}, u32[]{:S(2)}) collective-permute-start(bf16[112,384]{1,0:T(8,128)(2,1)S(1)} %fusion.4), channel_id=1, source_target_pairs={{0,16},{16,0},{1,17},{17,1},{2,18},{18,2},{3,19},{19,3},{4,20},{20... | collective-permute-start | bytes 258056 | tf_op jit(solution)/shard_map/ppermute | solution.py:123
  6.6 1.2 %copy-start.2 = (bf16[112,384]{1,0:T(8,128)(2,1)}, bf16[112,384]{1,0:T(8,128)(2,1)S(1)}, u32[]{:S(2)}) copy-start(bf16[112,384]{1,0:T(8,128)(2,1)S(1)} %fusion.5.own_ref) | copy-start | bytes 258052
  7.5 0.6 copy-start.4
  27.3 26.8 %copy-start = (f32[4,112,384]{2,1,0:T(8,128)S(1)}, f32[4,112,384]{2,1,0:T(8,128)}, u32[]{:S(2)}) copy-start(f32[4,112,384]{2,1,0:T(8,128)} %param.3) | copy-start | bytes 2064388
  51.1 5.6 %copy-start.5 = (bf16[112,384]{1,0:T(8,128)(2,1)S(1)}, bf16[112,384]{1,0:T(8,128)(2,1)}, u32[]{:S(2)}) copy-start(bf16[112,384]{1,0:T(8,128)(2,1)} %get-tuple-element.8) | copy-start | bytes 258052
  51.1 5.6 %collective-permute-start.1 = (bf16[112,384]{1,0:T(8,128)(2,1)}, bf16[112,384]{1,0:T(8,128)(2,1)S(1)}, u32[]{:S(2)}, u32[]{:S(2)}) collective-permute-start(bf16[112,384]{1,0:T(8,128)(2,1)} %get-tuple-element.9), channel_id=1, source_target_pairs={{0,16},{16,0},{1,17},{17,1},{2,18},{18,2},{3,19},{19,3},{4,20},{20... | collective-permute-start | bytes 258056 | tf_op jit(solution)/shard_map/ppermute | solution.py:136
  56.7 6.5 %copy-start.3 = (bf16[4,112,384]{2,1,0:T(8,128)(2,1)S(1)}, bf16[4,112,384]{2,1,0:T(8,128)(2,1)}, u32[]{:S(2)}) copy-start(bf16[4,112,384]{2,1,0:T(8,128)(2,1)} %param.5) | copy-start | bytes 1032196
